TPU v7x, 512 devices: a whole 4x4x16 slice. The times are simulated.
512 devices in a mesh: shape: 16 (over z_lo, x), query: 32 (over z_hi, y, core).
Axes of the slice: x: 4, y: 4, z: 16 (z_hi: 4, z_lo: 4; z = z_hi * 4 + z_lo), core: 2. Of those that a mesh axis runs over, the one named last changes fastest.
Arguments:
- queries: bfloat16 [16, 4096, 512], P('shape', 'query'), may hold values from -128 to 128
- keys: bfloat16 [16, 1024, 512], P('shape', 'query'), may hold values from -5 to 5
- values: bfloat16 [16, 1024, 512], P('shape', 'query'), may hold values from -6 to 6
- out_weight: bfloat16 [512, 512], replicated, may hold values from -0.25 to 0.25
- out_grad: float32 [16, 4096, 512], P('shape', 'query'), may hold values from -6 to 6
Outputs:
- query_grad: float32 [16, 4096, 512], P('shape', 'query')
- key_grad: float32 [16, 1024, 512], P('shape', 'query')
- value_grad: float32 [16, 1024, 512], P('shape', 'query')
- weight_grad: float32 [512, 512], replicated
All inputs are finite; a program needn't handle non-finite values.
Results may differ from a plain program's by a relative error of at most 0.02.
Values may be sent and summed in bfloat16 or wider, within the bound.
A program may use at most 64 MiB of HBM per device.

v0:
```python
import math

import jax
import jax.numpy as jnp
from jax import lax
from jax.sharding import PartitionSpec as P

HEADS = 8
HEAD = 64


def shards(queries, keys, values, out_weight, out_grad):
    lat_rows = keys.shape[1]
    width = queries.shape[2]
    scale = 1.0 / math.sqrt(HEAD)
    shape_count = lax.axis_size("shape")
    members = lax.axis_size("query")
    query_rows = queries[0]
    grad_b = out_grad[0].astype(jnp.bfloat16)
    d_attn = jnp.einsum("tf,df->td", grad_b, out_weight, preferred_element_type=jnp.float32).astype(
        jnp.bfloat16
    )
    key_all, value_all = (
        lax.all_gather(keys[0], "query", axis=0, tiled=True),
        lax.all_gather(values[0], "query", axis=0, tiled=True),
    )
    grad_list, attn_list, key_list, value_list = ([], [], [], [])
    for head_index in range(HEADS):
        cols = slice(head_index * HEAD, (head_index + 1) * HEAD)
        q_head = query_rows[:, cols]
        key_head = key_all[:, cols]
        value_head = value_all[:, cols]
        scores = jnp.dot(q_head, key_head.T, preferred_element_type=jnp.float32) * scale
        top = jnp.max(scores, axis=1, keepdims=True)
        lse = top + jnp.log(jnp.sum(jnp.exp(scores - top), axis=1, keepdims=True))
        probs = jnp.exp(scores - lse)
        probs_b = probs.astype(jnp.bfloat16)
        attn_b = jnp.dot(probs_b, value_head, preferred_element_type=jnp.float32).astype(
            jnp.bfloat16
        )
        d_head = d_attn[:, cols]
        delta = jnp.sum(
            d_head.astype(jnp.float32) * attn_b.astype(jnp.float32), axis=1, keepdims=True
        )
        d_probs = jnp.dot(d_head, value_head.T, preferred_element_type=jnp.float32)
        d_scores = (probs * (d_probs - delta) * scale).astype(jnp.bfloat16)
        grad_list.append(jnp.dot(d_scores, key_head, preferred_element_type=jnp.float32))
        key_list.append(
            jnp.einsum("tm,td->md", d_scores, q_head, preferred_element_type=jnp.float32)
        )
        value_list.append(
            jnp.einsum("tm,td->md", probs_b, d_head, preferred_element_type=jnp.float32)
        )
        attn_list.append(attn_b)
    query_grad = jnp.concatenate(grad_list, axis=1)
    attn = jnp.concatenate(attn_list, axis=1)
    key_terms = jnp.concatenate(key_list, axis=1).reshape(members, lat_rows, width)
    value_terms = jnp.concatenate(value_list, axis=1).reshape(members, lat_rows, width)
    key_in, value_in = (
        lax.all_to_all(key_terms, "query", split_axis=0, concat_axis=0, tiled=True),
        lax.all_to_all(value_terms, "query", split_axis=0, concat_axis=0, tiled=True),
    )
    key_grad = jnp.sum(key_in, axis=0)
    value_grad = jnp.sum(value_in, axis=0)
    weight_term = jnp.einsum("td,tf->df", attn, grad_b, preferred_element_type=jnp.float32) * (
        1.0 / shape_count
    )
    weight_grad = lax.psum(weight_term, ("shape", "query"))
    return (query_grad[None], key_grad[None], value_grad[None], weight_grad)


def solution(mesh):
    return jax.shard_map(
        shards,
        mesh=mesh,
        in_specs=(
            P("shape", "query", None),
            P("shape", "query", None),
            P("shape", "query", None),
            P(),
            P("shape", "query", None),
        ),
        out_specs=(
            P("shape", "query", None),
            P("shape", "query", None),
            P("shape", "query", None),
            P(),
        ),
        check_vma=False,
    )
```

profile of v0, /device:TPU:1, one launch (start us, length us, event | category | flops | bytes accessed | tf_op | source)
XLA Modules:
  0.0 804.2 jit_solution(14749125188669435958)
XLA Ops:
  8.2 1.3 convolution_convert_fusion
  9.5 79.2 %all-gather.5.cloned.1.call-done = bf16[1,1024,512]{2,1,0:T(8,128)(2,1)} async-done(((bf16[1,32,512]{2,1,0:T(8,128)(2,1)}), bf16[1,1024,512]{2,1,0:T(8,128)(2,1)}) %all-gather.5.cloned.1.call-update) | async-done | bytes 1048592 | tf_op jit(solution)/shard_map/all_gather | solution.py:24
  88.7 1.4 fusion.117
  90.1 1.6 fusion.118
  91.6 1.5 fusion.119
  100.0 1.0 convolution_dynamic-update-slice_fusion.4
  102.0 1.0 convolution_dynamic-update-slice_fusion.2
  105.0 2.9 copy.27
  107.9 7.5 all-to-all-start.1
  116.1 140.1 %all-gather.7.cloned.1.call-done = bf16[1,1024,512]{2,1,0:T(8,128)(2,1)} async-done(((bf16[1,32,512]{2,1,0:T(8,128)(2,1)}), bf16[1,1024,512]{2,1,0:T(8,128)(2,1)}) %all-gather.7.cloned.1.call-update) | async-done | bytes 1048592 | tf_op jit(solution)/shard_map/all_gather | solution.py:25
  256.3 1.4 convolution_convert_fusion.2
  257.7 1.3 convolution_convert_fusion.3
  259.1 1.3 convolution_convert_fusion.4
  267.5 1.0 convolution_dynamic-update-slice_fusion.12
  272.6 1.0 convolution_dynamic-update-slice_fusion.8
  273.6 2.9 copy.26
  276.7 7.6 all-to-all-start
  284.8 2.3 convolution_multiply_fusion
  290.4 1.8 copy.28
  292.2 2.4 reduce_sum.179
  294.5 90.0 %all-to-all-done = f32[32,32,512]{2,1,0:T(8,128)} async-done(((f32[32,32,512]{2,1,0:T(8,128)}), f32[32,32,512]{2,1,0:T(8,128)}, u32[]{:S(2)}, u32[]{:S(2)}) %all-to-all-start) | async-done | bytes 2097184 | tf_op jit(solution)/shard_map/all_to_all | solution.py:60
  384.6 2.4 reduce_sum.178
  386.9 408.5 %all-reduce.2.cloned.1.call-done = f32[512,512]{1,0:T(8,128)} async-done(((f32[512,512]{1,0:T(8,128)}), f32[512,512]{1,0:T(8,128)}) %all-reduce.2.cloned.1.call-update) | async-done | bytes 1048592 | tf_op jit(solution)/shard_map/psum | solution.py:68
  795.4 2.3 copy.59
  (158 shorter events, 26.0 us)
Async XLA Ops:
  7.2 84.4 %copy-start.23 = (bf16[1,128,512]{2,1,0:T(8,128)(2,1)S(1)}, bf16[1,128,512]{2,1,0:T(8,128)(2,1)}, u32[]{:S(2)}) copy-start(bf16[1,128,512]{2,1,0:T(8,128)(2,1)} %param.5) | copy-start | bytes 393220
  7.2 81.5 %all-gather.5.cloned.1.call-start = ((), (), s32[]{:S(2)}) async-start(), calls=%async_computation.3 | async-start | bytes 1081344 | tf_op jit(solution)/shard_map/all_gather | solution.py:24
  90.0 6.9 copy-start.9
  91.6 6.4 copy-start.7
  93.1 5.9 copy-start.5
  93.5 6.5 copy-start.3
  95.0 9.0 %copy-start.11 = (f32[128,1024]{1,0:T(8,128)}, f32[128,1024]{1,0:T(8,128)S(1)}, u32[]{:S(2)}) copy-start(f32[128,1024]{1,0:T(8,128)S(1)} %get-tuple-element.21) | copy-start | bytes 1572868
  95.2 166.2 %copy-start.43 = (f32[128]{0:T(128)}, f32[128]{0:T(128)S(1)}, u32[]{:S(2)}) copy-start(f32[128]{0:T(128)S(1)} %log_add_fusion.7) | copy-start | bytes 1540
  95.5 165.6 %copy-start.44 = (f32[128]{0:T(128)}, f32[128]{0:T(128)S(1)}, u32[]{:S(2)}) copy-start(f32[128]{0:T(128)S(1)} %log_add_fusion.6) | copy-start | bytes 1540
  95.7 165.0 %copy-start.41 = (f32[128]{0:T(128)}, f32[128]{0:T(128)S(1)}, u32[]{:S(2)}) copy-start(f32[128]{0:T(128)S(1)} %log_add_fusion.5) | copy-start | bytes 1540
  97.0 164.8 %copy-start.46 = (f32[128]{0:T(128)}, f32[128]{0:T(128)S(1)}, u32[]{:S(2)}) copy-start(f32[128]{0:T(128)S(1)} %log_add_fusion) | copy-start | bytes 1540
  107.9 168.7 %all-to-all-start.1 = ((f32[32,32,512]{2,1,0:T(8,128)}), f32[32,32,512]{2,1,0:T(8,128)}, u32[]{:S(2)}, u32[]{:S(2)}) async-start(f32[32,32,512]{2,1,0:T(8,128)} %bitcast.63), calls=%async_computation.1 | async-start | bytes 4194304 | tf_op jit(solution)/shard_map/all_to_all | solution.py:61
  115.4 140.9 %all-gather.7.cloned.1.call-start = ((), (), s32[]{:S(2)}) async-start(), calls=%async_computation.4 | async-start | bytes 1081344 | tf_op jit(solution)/shard_map/all_gather | solution.py:25
  256.3 4.8 copy-start.8
  276.6 8.0 copy-start.27
  276.6 8.0 copy-start.29
  276.6 8.0 copy-start.31
  276.6 8.0 copy-start.33
  276.6 8.0 copy-start.35
  276.6 8.0 copy-start.37
  276.6 8.0 copy-start.39
  276.6 8.0 copy-start.40
  276.7 107.9 %all-to-all-start = ((f32[32,32,512]{2,1,0:T(8,128)}), f32[32,32,512]{2,1,0:T(8,128)}, u32[]{:S(2)}, u32[]{:S(2)}) async-start(f32[32,32,512]{2,1,0:T(8,128)} %bitcast.64), calls=%async_computation | async-start | bytes 4194304 | tf_op jit(solution)/shard_map/all_to_all | solution.py:60
  284.3 511.1 %all-reduce.2.cloned.1.call-start = ((), (), s32[]{:S(2)}) async-start(), calls=%async_computation.2 | async-start | bytes 2097152 | tf_op jit(solution)/shard_map/psum | solution.py:68
  (29 other events, 98.1 us)
Sparse Core Ops, SparseCore 0:
  11.2 77.4 all-gather.4
  119.4 136.8 all-gather.6
  291.2 504.1 all-reduce.1
where the time goes:
time: 805 us; the launch traced here: 804 us
  waiting for transfers between devices  719 us (89%)
  matrix products  37.1 us (5%)
  starting transfers between devices  15.4 us (2%)
  between operations  14.6 us (2%)
  local copies, waits for them, and re-layouts  11.2 us (1%)
    psum x1, waiting for transfers between devices, shards(): weight_grad = lax.psum(weight_term, ('shape', 'query'))  408 us
    all_gather x1, waiting for transfers between devices, shards(): lax.all_gather(values[0], 'query', axis=0, tiled=True)  140 us
    all_to_all x1, waiting for transfers between devices, shards(): lax.all_to_all(key_terms, 'query', split_axis=0, concat_axis=0, tiled=True)  90 us
    all_gather x1, waiting for transfers between devices, shards(): lax.all_gather(keys[0], 'query', axis=0, tiled=True)  79.2 us
  transfers between devices with their start and end apart: 5, of which 4 were waited for; matrix products, arithmetic and copies ran while one was open for 4% of the time, Pallas kernels for 0%

commit v1 on v0

v1 whole, which is shorter than its diff:
```python
import math

import jax
import jax.numpy as jnp
from jax import lax
from jax.experimental import pallas as pl
from jax.experimental.pallas import tpu as pltpu
from jax.sharding import PartitionSpec as P

MESH = pl.DeviceIdType.MESH
BF = jnp.bfloat16
F32 = jnp.float32

ROWS = 128
LAT = 32
D = 512
HALF = 256
SHAPES = 16
SCALE = 1.0 / math.sqrt(64)
LOG2E = 1.4426950408889634


def nt(a, b):
    return lax.dot_general(a, b, (((1,), (1,)), ((), ())), preferred_element_type=F32)


def tn(a, b):
    return lax.dot_general(a, b, (((0,), (0,)), ((), ())), preferred_element_type=F32)


def nn(a, b):
    return lax.dot_general(a, b, (((1,), (0,)), ((), ())), preferred_element_type=F32)


def kernel(
    q_hbm, k_hbm, v_hbm, w_hbm, g_hbm,
    dq_out, dk_out, dv_out, dw_out,
    kv, q2, gb, gst, w_v, dat, da, s_ref, pb_ref, ds_ref, at, qbd, dbd, qst, dst,
    dkv, ry, rz, red, fin, dqs, wpart, w_a, w_b_src, w_b, w_c,
    loc, sib_s, sib_r, ag_s, ag_r, ry_s, ry_r, rz_s, rz_r, fin_s, fin_r, dq_s, dq_r,
    a_s, a_r, b_s, b_r, c_s, c_r, d_s, d_r, e_s, e_r,
):
    shape_at = lax.axis_index("shape")
    query_at = lax.axis_index("query")
    core = lax.rem(query_at, 2)
    other = 1 - core
    y = lax.rem(lax.div(query_at, 2), 4)
    zh = lax.div(query_at, 8)
    x = lax.rem(shape_at, 4)
    zl = lax.div(shape_at, 4)
    y1, y2, y3 = [lax.rem(y + i, 4) for i in (1, 2, 3)]
    z1, z2, z3 = [lax.rem(zh + i, 4) for i in (1, 2, 3)]
    sib = (shape_at, query_at + 1 - 2 * core)
    to_z = {1: (shape_at, z1 * 8 + y * 2 + core), -1: (shape_at, z3 * 8 + y * 2 + core)}
    to_y = {1: (shape_at, zh * 8 + y1 * 2 + core), -1: (shape_at, zh * 8 + y3 * 2 + core)}
    plane = x * 4 + y
    line = zh * 4 + zl

    def plane_peer(i):
        return (zl * 4 + lax.div(i, 4), zh * 8 + lax.rem(i, 4) * 2 + core)

    def line_peer(i):
        return (lax.rem(i, 4) * 4 + x, lax.div(i, 4) * 8 + y * 2 + core)

    barrier = pltpu.get_barrier_semaphore()
    pl.semaphore_signal(barrier, inc=1, device_id=sib, device_id_type=MESH)

    @pl.loop(1, 16)
    def _(i):
        pl.semaphore_signal(barrier, inc=1, device_id=line_peer(lax.rem(line + i, 16)), device_id_type=MESH)
        pl.semaphore_signal(barrier, inc=1, device_id=plane_peer(lax.rem(plane + i, 16)), device_id_type=MESH)

    mine = pl.ds(pl.multiple_of(core * HALF, HALF), HALF)
    theirs = pl.ds(pl.multiple_of(other * HALF, HALF), HALF)
    my_rows = pl.ds(pl.multiple_of(core * ROWS, ROWS), ROWS)

    def block_cols(c, b):
        return pl.ds(pl.multiple_of(c * HALF + b * 128, 128), 128)

    local = [pltpu.make_async_copy(g_hbm, gst, loc.at[0])]
    for b in range(2):
        for t, ref in enumerate((k_hbm, v_hbm)):
            local.append(
                pltpu.make_async_copy(ref.at[:, block_cols(core, b)], kv.at[b, zh, y, core, t], loc.at[1 + 2 * b + t])
            )
    local.append(pltpu.make_async_copy(w_hbm.at[mine, :], w_v, loc.at[5]))
    local.append(pltpu.make_async_copy(q_hbm.at[:, mine], q2.at[my_rows, :], loc.at[6]))
    for c in local:
        c.start()
    local[0].wait()
    gb[my_rows, :] = gst[...].astype(BF)

    sends = []

    def send(src, dst, ss, rs, dev):
        c = pltpu.make_async_remote_copy(
            src_ref=src, dst_ref=dst, send_sem=ss, recv_sem=rs, device_id=dev, device_id_type=MESH
        )
        c.start()
        sends.append(c)

    def got(ref, ss, rs):
        pltpu.make_async_remote_copy(
            src_ref=ref, dst_ref=ref, send_sem=ss, recv_sem=rs, device_id=sib, device_id_type=MESH
        ).wait_recv()

    pl.semaphore_wait(barrier, 31)

    for b in range(2):
        for t, ref in enumerate((k_hbm, v_hbm)):
            send(ref.at[:, block_cols(other, b)], kv.at[b, zh, y, core, t], sib_s.at[2 * b + t], sib_r.at[2 * b + t], sib)
    send(gb.at[my_rows, :], gb.at[my_rows, :], sib_s.at[4], sib_r.at[4], sib)
    send(q_hbm.at[:, theirs], q2.at[my_rows, :], sib_s.at[5], sib_r.at[5], sib)

    def sub(z, yy, c):
        return kv.at[:, z, yy, c]

    def piece(z, yy):
        return kv.at[:, z, yy]

    def ag_send(ref, z, yy, c, slot, dev):
        send(ref, ref, ag_s.at[z, yy, c, slot], ag_r.at[z, yy, c], dev)

    def ag_got(ref, z, yy, c):
        got(ref, ag_s.at[z, yy, c, 0], ag_r.at[z, yy, c])

    for c in local[1:5]:
        c.wait()
    for c in (core, other):
        if c is other:
            for b in range(2):
                for t in range(2):
                    got(kv.at[b, zh, y, other, t], sib_s.at[2 * b + t], sib_r.at[2 * b + t])
        ag_send(sub(zh, y, c), zh, y, c, 0, to_z[1])
        ag_send(sub(zh, y, c), zh, y, c, 1, to_z[-1])
        ag_send(sub(zh, y, c), zh, y, c, 2, to_y[1])
        ag_send(sub(zh, y, c), zh, y, c, 3, to_y[-1])
    for c in local[5:]:
        c.wait()
    got(gb.at[pl.ds(pl.multiple_of(other * ROWS, ROWS), ROWS), :], sib_s.at[4], sib_r.at[4])
    got(q2.at[pl.ds(pl.multiple_of(other * ROWS, ROWS), ROWS), :], sib_s.at[5], sib_r.at[5])

    ag_got(sub(z3, y, 0), z3, y, 0)
    ag_send(sub(z3, y, 0), z3, y, 0, 0, to_z[1])
    ag_got(sub(z1, y, 1), z1, y, 1)
    ag_send(sub(z1, y, 1), z1, y, 1, 1, to_z[-1])
    ag_got(sub(z3, y, 1), z3, y, 1)
    ag_send(piece(z3, y), z3, y, 0, 2, to_y[1])
    ag_send(piece(z3, y), z3, y, 0, 3, to_y[-1])
    ag_got(sub(z1, y, 0), z1, y, 0)
    ag_send(piece(z1, y), z1, y, 0, 2, to_y[1])
    ag_send(piece(z1, y), z1, y, 0, 3, to_y[-1])
    ag_got(sub(zh, y3, 0), zh, y3, 0)
    ag_send(sub(zh, y3, 0), zh, y3, 0, 2, to_y[1])
    ag_got(sub(zh, y1, 1), zh, y1, 1)
    ag_send(sub(zh, y1, 1), zh, y1, 1, 3, to_y[-1])

    dat[...] = nt(w_v[...], gb[...]).astype(BF)
    da[...] = nt(gb[...], w_v[...]).astype(BF)

    ag_got(sub(z2, y, 0), z2, y, 0)
    ag_got(sub(z2, y, 1), z2, y, 1)
    ag_send(piece(z2, y), z2, y, 0, 2, to_y[1])
    ag_send(piece(z2, y), z2, y, 0, 3, to_y[-1])
    for z in (z3, z1, z2):
        ag_got(piece(z, y3), z, y3, 0)
        ag_send(sub(z, y3, 0), z, y3, 0, 2, to_y[1])
        ag_got(piece(z, y1), z, y1, 0)
        ag_send(sub(z, y1, 1), z, y1, 1, 3, to_y[-1])
    ag_got(sub(zh, y3, 1), zh, y3, 1)
    ag_got(sub(zh, y1, 0), zh, y1, 0)
    for z in (zh, z3, z1, z2):
        for c in range(2):
            ag_got(sub(z, y2, c), z, y2, c)

    def keys_of(b, z):
        return kv[b, z, :, :, 0].reshape(256, 128)

    def values_of(b, z):
        return kv[b, z, :, :, 1].reshape(256, 128)

    def all_of(b, t):
        return kv[b, :, :, :, t].reshape(1024, 128)

    low = lax.broadcasted_iota(jnp.int32, (256, 128), 1) < 64
    zero = jnp.zeros((64, 256), BF)

    def forward(b):
        cols = slice(b * 128, b * 128 + 128)
        q_t = q2[:, cols].T
        qbd[0:64, 0:256] = q_t[0:64]
        qbd[0:64, 256:512] = zero
        qbd[64:128, 0:256] = zero
        qbd[64:128, 256:512] = q_t[64:128]
        top = None
        for r in range(4):
            s = nn(keys_of(b, r), qbd[...])
            s_ref[b, r] = s
            m = jnp.max(s, axis=0, keepdims=True)
            top = m if top is None else jnp.maximum(top, m)
        total = None
        for r in range(4):
            e = jnp.exp2((s_ref[b, r] - top) * (SCALE * LOG2E))
            s_ref[b, r] = e
            m = jnp.sum(e, axis=0, keepdims=True)
            total = m if total is None else total + m
        inv = 1.0 / total
        for r in range(4):
            p = s_ref[b, r] * inv
            s_ref[b, r] = p
            pb_ref[b, r * 256 : r * 256 + 256] = p.astype(BF)
        a = tn(all_of(b, 1), pb_ref[b])
        at[b * 128 : b * 128 + 64, :] = a[0:64, 0:256].astype(BF)
        at[b * 128 + 64 : b * 128 + 128, :] = a[64:128, 256:512].astype(BF)

    def backward(b):
        cols = slice(b * 128, b * 128 + 128)
        prod = dat[cols, :].astype(F32) * at[cols, :].astype(F32)
        delta = jnp.concatenate(
            [jnp.sum(prod[0:64], axis=0, keepdims=True), jnp.sum(prod[64:128], axis=0, keepdims=True)], axis=1
        )
        dbd[0:64, 0:256] = dat[b * 128 : b * 128 + 64, :]
        dbd[0:64, 256:512] = zero
        dbd[64:128, 0:256] = zero
        dbd[64:128, 256:512] = dat[b * 128 + 64 : b * 128 + 128, :]
        none = jnp.zeros((256, 128), BF)
        qst[0:256] = jnp.where(low, q2[:, cols], none)
        qst[256:512] = jnp.where(low, none, q2[:, cols])
        dst[0:256] = jnp.where(low, da[:, cols], none)
        dst[256:512] = jnp.where(low, none, da[:, cols])
        for r in range(4):
            dp = nn(values_of(b, r), dbd[...])
            ds = (s_ref[b, r] * (dp - delta)).astype(BF)
            ds_ref[r * 256 : r * 256 + 256] = ds
            dkv[b, r, :, :, 0] = (nn(ds, qst[...]) * SCALE).astype(BF).reshape(4, 2, LAT, 128)
            dkv[b, r, :, :, 1] = nn(pb_ref[b, r * 256 : r * 256 + 256], dst[...]).astype(BF).reshape(4, 2, LAT, 128)

    def query_part(b):
        a = tn(all_of(b, 0), ds_ref[...]) * SCALE
        for c in range(2):
            rows = slice(c * 128, c * 128 + 128)
            dqs[b, c] = jnp.concatenate([a[0:64, rows], a[64:128, 256 + c * 128 : 384 + c * 128]], axis=0).T
        dq_out[:, block_cols(core, b)] = dqs[b, core]
        send(dqs.at[b, other], dq_out.at[:, block_cols(core, b)], dq_s.at[b], dq_r.at[b], sib)

    def rs_y_start(b):
        send(dkv.at[b, :, y2, 0], ry.at[b, 0, 0], ry_s.at[b, 0, 0], ry_r.at[b, 0, 0], to_y[1])
        send(dkv.at[b, :, y2, 1], ry.at[b, 1, 0], ry_s.at[b, 1, 0], ry_r.at[b, 1, 0], to_y[-1])
        send(dkv.at[b, :, y1, 1], ry.at[b, 0, 1], ry_s.at[b, 0, 1], ry_r.at[b, 0, 1], to_y[1])
        send(dkv.at[b, :, y3, 0], ry.at[b, 1, 1], ry_s.at[b, 1, 1], ry_r.at[b, 1, 1], to_y[-1])

    def add(*parts):
        out = parts[0].astype(F32)
        for p in parts[1:]:
            out = out + p.astype(F32)
        return out

    def rs_y_middle(b):
        got(ry.at[b, 0, 0], ry_s.at[b, 0, 0], ry_r.at[b, 0, 0])
        dkv[b, :, y1, 0] = add(dkv[b, :, y1, 0], ry[b, 0, 0]).astype(BF)
        send(dkv.at[b, :, y1, 0], ry.at[b, 0, 2], ry_s.at[b, 0, 2], ry_r.at[b, 0, 2], to_y[1])
        got(ry.at[b, 1, 0], ry_s.at[b, 1, 0], ry_r.at[b, 1, 0])
        dkv[b, :, y3, 1] = add(dkv[b, :, y3, 1], ry[b, 1, 0]).astype(BF)
        send(dkv.at[b, :, y3, 1], ry.at[b, 1, 2], ry_s.at[b, 1, 2], ry_r.at[b, 1, 2], to_y[-1])

    def rs_z_start(b):
        for i in range(2):
            for k in (1, 2):
                got(ry.at[b, i, k], ry_s.at[b, i, k], ry_r.at[b, i, k])
        red[b, :, 0] = add(dkv[b, :, y, 0], ry[b, 0, 2], ry[b, 1, 1]).astype(BF)
        red[b, :, 1] = add(dkv[b, :, y, 1], ry[b, 0, 1], ry[b, 1, 2]).astype(BF)
        send(red.at[b, z2, 0], rz.at[b, 0, 0], rz_s.at[b, 0, 0], rz_r.at[b, 0, 0], to_z[1])
        send(red.at[b, z2, 1], rz.at[b, 1, 0], rz_s.at[b, 1, 0], rz_r.at[b, 1, 0], to_z[-1])
        send(red.at[b, z1, 1], rz.at[b, 0, 1], rz_s.at[b, 0, 1], rz_r.at[b, 0, 1], to_z[1])
        send(red.at[b, z3, 0], rz.at[b, 1, 1], rz_s.at[b, 1, 1], rz_r.at[b, 1, 1], to_z[-1])

    def rs_z_middle(b):
        got(rz.at[b, 0, 0], rz_s.at[b, 0, 0], rz_r.at[b, 0, 0])
        red[b, z1, 0] = add(red[b, z1, 0], rz[b, 0, 0]).astype(BF)
        send(red.at[b, z1, 0], rz.at[b, 0, 2], rz_s.at[b, 0, 2], rz_r.at[b, 0, 2], to_z[1])
        got(rz.at[b, 1, 0], rz_s.at[b, 1, 0], rz_r.at[b, 1, 0])
        red[b, z3, 1] = add(red[b, z3, 1], rz[b, 1, 0]).astype(BF)
        send(red.at[b, z3, 1], rz.at[b, 1, 2], rz_s.at[b, 1, 2], rz_r.at[b, 1, 2], to_z[-1])

    def rs_end(b):
        for i in range(2):
            for k in (1, 2):
                got(rz.at[b, i, k], rz_s.at[b, i, k], rz_r.at[b, i, k])
        fin[b, 0] = add(red[b, zh, 0], rz[b, 0, 2], rz[b, 1, 1])
        fin[b, 1] = add(red[b, zh, 1], rz[b, 0, 1], rz[b, 1, 2])
        for t, out in enumerate((dk_out, dv_out)):
            send(fin.at[b, other, t], out.at[:, block_cols(core, b)], fin_s.at[b, t], fin_r.at[b, t], sib)
            out[:, block_cols(core, b)] = fin[b, core, t]

    def fin_got(b):
        for t, out in enumerate((dk_out, dv_out)):
            got(out.at[:, block_cols(other, b)], fin_s.at[b, t], fin_r.at[b, t])
        got(dq_out.at[:, block_cols(other, b)], dq_s.at[b], dq_r.at[b])

    def loop_copies(make, how):
        @pl.loop(1, 16)
        def _(i):
            c = make(i)
            getattr(c, how)()

    def remote(src, dst, ss, rs, dev):
        return pltpu.make_async_remote_copy(
            src_ref=src, dst_ref=dst, send_sem=ss, recv_sem=rs, device_id=dev, device_id_type=MESH
        )

    def a_copy(i):
        peer = lax.rem(plane + i, 16)
        return remote(wpart.at[peer], w_a.at[plane], a_s.at[peer], a_r.at[plane], plane_peer(peer))

    def a_in(i):
        return remote(w_a.at[i], w_a.at[i], a_s.at[i], a_r.at[i], sib)

    def b_copy(i):
        peer = lax.rem(line + i, 16)
        return remote(w_b_src.at[lax.rem(peer, 4)], w_b.at[line], b_s.at[peer], b_r.at[line], line_peer(peer))

    def b_in(i):
        return remote(w_b.at[i], w_b.at[i], b_s.at[i], b_r.at[i], sib)

    def d_copy(i):
        peer = lax.rem(plane + i, 16)
        return remote(dw_out.at[core, plane], dw_out.at[core, plane], d_s.at[peer], d_r.at[plane], plane_peer(peer))

    def d_in(i):
        return remote(dw_out.at[core, i], dw_out.at[core, i], d_s.at[i], d_r.at[i], sib)

    def w_start():
        wpart[...] = nn(at[...], gb[...]).astype(BF).reshape(16, 16, D)
        w_a[plane] = wpart[plane]
        loop_copies(a_copy, "start")

    def w_line():
        loop_copies(lambda i: a_in(lax.rem(plane + i, 16)), "wait_recv")
        total = jnp.sum(w_a[...].astype(F32), axis=0)
        for p in range(4):
            w_b_src[p] = total[:, p * 128 : p * 128 + 128].astype(BF)
        w_b[line] = w_b_src[zl]
        loop_copies(b_copy, "start")

    def w_near():
        loop_copies(lambda i: b_in(lax.rem(line + i, 16)), "wait_recv")
        w_c[zl] = (jnp.sum(w_b[...].astype(F32), axis=0) * (1.0 / SHAPES)).astype(BF)
        for k in (1, 2, 3):
            peer = lax.rem(zl + k, 4)
            send(w_c.at[zl], w_c.at[zl], c_s.at[peer], c_r.at[zl], line_peer(zh * 4 + peer))

    def w_plane():
        for k in (1, 2, 3):
            peer = lax.rem(zl + k, 4)
            got(w_c.at[peer], c_s.at[peer], c_r.at[peer])
        for p in range(4):
            dw_out[core, plane, :, p * 128 : p * 128 + 128] = w_c[p]
        loop_copies(d_copy, "start")

    def w_pair():
        loop_copies(lambda i: d_in(lax.rem(plane + i, 16)), "wait_recv")
        send(dw_out.at[core], dw_out.at[core], e_s, e_r, sib)

    def w_end():
        got(dw_out.at[other], e_s, e_r)
        loop_copies(a_copy, "wait_send")
        loop_copies(b_copy, "wait_send")
        loop_copies(d_copy, "wait_send")

    forward(0)
    forward(1)
    w_start()
    backward(0)
    rs_y_start(0)
    query_part(0)
    rs_y_middle(0)
    w_line()
    backward(1)
    rs_y_start(1)
    rs_z_start(0)
    query_part(1)
    w_near()
    rs_y_middle(1)
    rs_z_middle(0)
    w_plane()
    rs_z_start(1)
    rs_end(0)
    rs_z_middle(1)
    w_pair()
    rs_end(1)
    w_end()
    fin_got(0)
    fin_got(1)
    for c in sends:
        c.wait_send()


def shards(queries, keys, values, out_weight, out_grad):
    dma = pltpu.SemaphoreType.DMA
    vm = pltpu.VMEM
    dq, dk, dv, dw = pl.pallas_call(
        kernel,
        out_shape=(
            jax.ShapeDtypeStruct((ROWS, D), F32),
            jax.ShapeDtypeStruct((LAT, D), F32),
            jax.ShapeDtypeStruct((LAT, D), F32),
            jax.ShapeDtypeStruct((2, 16, 16, D), BF),
        ),
        in_specs=[pl.BlockSpec(memory_space=pl.ANY)] * 5,
        out_specs=[pl.BlockSpec(memory_space=pltpu.VMEM)] * 4,
        scratch_shapes=[
            vm((2, 4, 4, 2, 2, LAT, 128), BF),
            vm((256, 256), BF),
            vm((256, D), BF),
            vm((ROWS, D), F32),
            vm((256, D), BF),
            vm((256, 256), BF),
            vm((256, 256), BF),
            vm((2, 4, 256, 512), F32),
            vm((2, 1024, 512), BF),
            vm((1024, 512), BF),
            vm((256, 256), BF),
            vm((128, 512), BF),
            vm((128, 512), BF),
            vm((512, 128), BF),
            vm((512, 128), BF),
            vm((2, 4, 4, 2, 2, LAT, 128), BF),
            vm((2, 2, 3, 4, 2, LAT, 128), BF),
            vm((2, 2, 3, 2, LAT, 128), BF),
            vm((2, 4, 2, 2, LAT, 128), BF),
            vm((2, 2, 2, LAT, 128), F32),
            vm((2, 2, 128, 128), F32),
            vm((16, 16, D), BF),
            vm((16, 16, D), BF),
            vm((4, 16, 128), BF),
            vm((16, 16, 128), BF),
            vm((4, 16, 128), BF),
            dma((7,)), dma((6,)), dma((6,)),
            dma((4, 4, 2, 4)), dma((4, 4, 2)),
            dma((2, 2, 3)), dma((2, 2, 3)), dma((2, 2, 3)), dma((2, 2, 3)),
            dma((2, 2)), dma((2, 2)), dma((2,)), dma((2,)),
            dma((16,)), dma((16,)), dma((16,)), dma((16,)), dma((4,)), dma((4,)), dma((16,)), dma((16,)),
            dma, dma,
        ],
        compiler_params=pltpu.CompilerParams(
            collective_id=0, has_side_effects=True, vmem_limit_bytes=48 * 1024 * 1024
        ),
        name="attend_back",
    )(queries[0], keys[0], values[0], out_weight, out_grad[0])
    return (dq[None], dk[None], dv[None], dw.reshape(D, D).astype(F32))


def solution(mesh):
    part = P("shape", "query", None)
    return jax.shard_map(
        shards,
        mesh=mesh,
        in_specs=(part, part, part, P(), part),
        out_specs=(part, part, part, P()),
        check_vma=False,
    )
```

time: 805 us -> 84.8 us (0.11)
  waiting for transfers between devices: 719 us -> 0 us
  Pallas kernels: 0 us -> 76.3 us
  matrix products: 37.1 us -> 0 us
  starting transfers between devices: 15.4 us -> 0 us
  between operations: 14.6 us -> 0.65 us
    psum x1 -> x0, waiting for transfers between devices: 408 us -> none  [shards(): weight_grad = lax.psum(weight_term, ('shape', 'query'))]
    all_gather x2 -> x0, waiting for transfers between devices: 219 us -> none  [the longest x1 140 us: shards(): lax.all_gather(values[0], 'query', axis=0, tiled=True)]
    all_to_all x2 -> x0, waiting for transfers between devices: 90 us -> none  [the longest x1 90 us: shards(): lax.all_to_all(key_terms, 'query', split_axis=0, concat_axis=0, tiled=True)]
    pallas_call x0 -> x1, Pallas kernels: none -> 76.3 us  [shards(): pl.pallas_call(kernel, out_shape=(jax.ShapeDtypeStruct((ROWS, D), F32), j...]
    dot_general x50 -> x0, matrix products: 37.1 us -> none  [the longest x8 7.99 us: shards(): jnp.einsum('tm,td->md', probs_b, d_head, preferred_element_type=jnp.float32)]
    all_to_all x2 -> x0, starting transfers between devices: 15.1 us -> none  [the longest x1 7.63 us: shards(): lax.all_to_all(key_terms, 'query', split_axis=0, concat_axis=0, tiled=True)]
  transfers between devices with their start and end apart: 5 -> 0, of which waited for: 4 -> 0; matrix products, arithmetic and copies ran while one was open for 4% -> 0% of each run, Pallas kernels for 0% -> 0%
where the time goes in v1:
time: 84.8 us; the launch traced here: 84.5 us
  Pallas kernels  76.3 us (90%)
  local copies, waits for them, and re-layouts  6.36 us (8%)
  other arithmetic  1.14 us (1%)
    pallas_call x1, Pallas kernels, shards(): pl.pallas_call(kernel, out_shape=(jax.ShapeDtypeStruct((ROWS, D), F32), j...  76.3 us
    unnamed x13, local copies, waits for them, and re-layouts  6.36 us

profile of v1, /device:TPU:1, one launch (start us, length us, event | category | flops | bytes accessed | tf_op | source)
XLA Modules:
  0.0 84.5 jit_solution(398415612013607298)
XLA Ops:
  0.6 0.0 copy-start
  0.6 1.0 %copy-done = bf16[512,512]{1,0:T(8,128)(2,1)S(1)} copy-done((bf16[512,512]{1,0:T(8,128)(2,1)S(1)}, bf16[512,512]{1,0:T(8,128)(2,1)}, u32[]{:S(2)}) %copy-start) | copy-done | bytes 524312
  1.7 0.0 copy-start.1
  1.7 0.9 %copy-done.1 = f32[1,128,512]{2,1,0:T(8,128)S(1)} copy-done((f32[1,128,512]{2,1,0:T(8,128)S(1)}, f32[1,128,512]{2,1,0:T(8,128)}, u32[]{:S(2)}) %copy-start.1) | copy-done | bytes 262168
  2.6 0.0 copy-start.2
  2.6 0.9 %copy-done.2 = bf16[1,128,512]{2,1,0:T(8,128)(2,1)S(1)} copy-done((bf16[1,128,512]{2,1,0:T(8,128)(2,1)S(1)}, bf16[1,128,512]{2,1,0:T(8,128)(2,1)}, u32[]{:S(2)}) %copy-start.2) | copy-done | bytes 131096
  3.5 0.0 copy-start.3
  3.5 0.8 copy-done.3
  4.3 0.0 copy-start.4
  4.3 0.8 copy-done.4
  5.0 76.3 %attend_back.1 = (f32[128,512]{1,0:T(8,128)S(1)}, f32[32,512]{1,0:T(8,128)S(1)}, f32[32,512]{1,0:T(8,128)S(1)}, bf16[2,16,16,512]{3,2,1,0:T(8,128)(2,1)S(1)}) custom-call(bf16[128,512]{1,0:T(8,128)(2,1)S(1)} %bitcast.12, bf16[32,512]{1,0:T(8,128)(2,1)S(1)} %bitcast.15, bf16[32,512]{1,0:T(8,128)(2,1)S(1)} %bitcast.16, bf16[512,512]{1,0:T(8,128)(2,1)S(1)} %copy-done, ...), custom_call_target="tpu_custom_call" | custom-call | tf_op jit(solution)/shard_map/attend_back/pallas_call | solution.py:401
  81.4 1.1 %bitcast_convert_fusion = f32[512,512]{1,0:T(8,128)} fusion(bf16[2,16,16,512]{3,2,1,0:T(8,128)(2,1)S(1)} %get-tuple-element.11), kind=kLoop, calls=%fused_computation | loop fusion | flops 262144 | bytes 1572864 | tf_op jit(solution)/shard_map/convert_element_type | solution.py:450
  82.5 0.7 copy.12
  83.2 0.6 copy.13
  83.9 0.6 copy.14
Async XLA Ops:
  0.6 1.0 %copy-start = (bf16[512,512]{1,0:T(8,128)(2,1)S(1)}, bf16[512,512]{1,0:T(8,128)(2,1)}, u32[]{:S(2)}) copy-start(bf16[512,512]{1,0:T(8,128)(2,1)} %w_hbm.1) | copy-start | bytes 1572868
  1.7 0.9 %copy-start.1 = (f32[1,128,512]{2,1,0:T(8,128)S(1)}, f32[1,128,512]{2,1,0:T(8,128)}, u32[]{:S(2)}) copy-start(f32[1,128,512]{2,1,0:T(8,128)} %param.9) | copy-start | bytes 786436
  2.6 0.9 %copy-start.2 = (bf16[1,128,512]{2,1,0:T(8,128)(2,1)S(1)}, bf16[1,128,512]{2,1,0:T(8,128)(2,1)}, u32[]{:S(2)}) copy-start(bf16[1,128,512]{2,1,0:T(8,128)(2,1)} %param.5) | copy-start | bytes 393220
  3.5 0.8 copy-start.3
  4.3 0.8 copy-start.4

commit v2 on v1

v2 whole, which is shorter than its diff:
```python
import math

import jax
import jax.numpy as jnp
from jax import lax
from jax.experimental import pallas as pl
from jax.experimental.pallas import tpu as pltpu
from jax.sharding import PartitionSpec as P

MESH = pl.DeviceIdType.MESH
BF = jnp.bfloat16
F32 = jnp.float32

ROWS = 128
LAT = 32
D = 512
HALF = 256
SHAPES = 16
SCALE = 1.0 / math.sqrt(64)
LOG2E = 1.4426950408889634


def nt(a, b):
    return lax.dot_general(a, b, (((1,), (1,)), ((), ())), preferred_element_type=F32)


def tn(a, b):
    return lax.dot_general(a, b, (((0,), (0,)), ((), ())), preferred_element_type=F32)


def nn(a, b):
    return lax.dot_general(a, b, (((1,), (0,)), ((), ())), preferred_element_type=F32)


def kernel(
    q_hbm, k_hbm, v_hbm, w_hbm, g_hbm,
    dq_out, dk_out, dv_out, dw_out,
    kv, q2, gb, gst, w_v, dat, da, s_ref, pb_ref, ds_ref, at, qbd, dbd, qst, dst,
    dkv, ry, rz, red, fin, dqs, wpart, w_a, w_b_src, w_b, w_c,
    loc, sib_s, sib_r, agz_s, agz_r, agy_s, agy_r, ry_s, ry_r, rz_s, rz_r, fin_s, fin_r, dq_s, dq_r,
    a_s, a_r, b_s, b_r, c_s, c_r, d_s, d_r, e_s, e_r,
):
    shape_at = lax.axis_index("shape")
    query_at = lax.axis_index("query")
    core = lax.rem(query_at, 2)
    other = 1 - core
    y = lax.rem(lax.div(query_at, 2), 4)
    zh = lax.div(query_at, 8)
    x = lax.rem(shape_at, 4)
    zl = lax.div(shape_at, 4)
    y1, y2, y3 = [lax.rem(y + i, 4) for i in (1, 2, 3)]
    z1, z2, z3 = [lax.rem(zh + i, 4) for i in (1, 2, 3)]
    sib = (shape_at, query_at + 1 - 2 * core)
    to_z = {1: (shape_at, z1 * 8 + y * 2 + core), -1: (shape_at, z3 * 8 + y * 2 + core)}
    to_y = {1: (shape_at, zh * 8 + y1 * 2 + core), -1: (shape_at, zh * 8 + y3 * 2 + core)}
    line = zh * 4 + zl
    plane = x * 4 + y

    def y_peer(i):
        return (shape_at, zh * 8 + i * 2 + core)

    def plane_peer(i):
        return (zl * 4 + lax.div(i, 4), zh * 8 + lax.rem(i, 4) * 2 + core)

    def line_peer(i):
        return (lax.rem(i, 4) * 4 + x, lax.div(i, 4) * 8 + y * 2 + core)

    def after(i, k):
        return lax.rem(i + k, 4)

    barrier = pltpu.get_barrier_semaphore()

    def greet(dev):
        pl.semaphore_signal(barrier, inc=1, device_id=dev, device_id_type=MESH)

    greet(to_z[1])
    greet(to_z[-1])
    for k in (1, 2, 3):
        greet(line_peer(zh * 4 + after(zl, k)))

    @pl.loop(1, 16)
    def _(i):
        greet(plane_peer(lax.rem(plane + i, 16)))

    greet(sib)

    mine = pl.ds(pl.multiple_of(core * HALF, HALF), HALF)
    theirs = pl.ds(pl.multiple_of(other * HALF, HALF), HALF)
    my_rows = pl.ds(pl.multiple_of(core * ROWS, ROWS), ROWS)

    def block_cols(c, b):
        return pl.ds(pl.multiple_of(c * HALF + b * 128, 128), 128)

    local = [pltpu.make_async_copy(g_hbm, gst, loc.at[0])]
    for b in range(2):
        for t, ref in enumerate((k_hbm, v_hbm)):
            local.append(
                pltpu.make_async_copy(ref.at[:, block_cols(core, b)], kv.at[b, zh, y, core, t], loc.at[1])
            )
    local.append(pltpu.make_async_copy(w_hbm.at[mine, :], w_v, loc.at[2]))
    local.append(pltpu.make_async_copy(q_hbm.at[:, mine], q2.at[my_rows, :], loc.at[3]))
    for c in local:
        c.start()
    local[0].wait()
    gb[my_rows, :] = gst[...].astype(BF)

    sends = []

    def remote(src, dst, ss, rs, dev):
        return pltpu.make_async_remote_copy(
            src_ref=src, dst_ref=dst, send_sem=ss, recv_sem=rs, device_id=dev, device_id_type=MESH
        )

    def send(src, dst, ss, rs, dev, wait=True):
        c = remote(src, dst, ss, rs, dev)
        c.start()
        if wait:
            sends.append(c)

    def got(ref, sem):
        remote(ref, ref, sem, sem, sib).wait_recv()

    def sent(ref, sem):
        remote(ref, ref, sem, sem, sib).wait_send()

    pl.semaphore_wait(barrier, 21)

    for b in range(2):
        for t, ref in enumerate((k_hbm, v_hbm)):
            send(ref.at[:, block_cols(other, b)], kv.at[b, zh, y, core, t], sib_s.at[0], sib_r.at[0], sib, False)
    send(gb.at[my_rows, :], gb.at[my_rows, :], sib_s.at[1], sib_r.at[1], sib)
    send(q_hbm.at[:, theirs], q2.at[my_rows, :], sib_s.at[2], sib_r.at[2], sib)

    low = lax.broadcasted_iota(jnp.int32, (256, 128), 1) < 64
    zero = jnp.zeros((64, 256), BF)

    def prepare(b):
        cols = slice(b * 128, b * 128 + 128)
        q_t = q2[:, cols].T
        for ref, part in ((qbd, q_t), (dbd, dat[cols, :])):
            ref[b, 0:64, 0:256] = part[0:64]
            ref[b, 0:64, 256:512] = zero
            ref[b, 64:128, 0:256] = zero
            ref[b, 64:128, 256:512] = part[64:128]
        none = jnp.zeros((256, 128), BF)
        for ref, part in ((qst, q2[:, cols]), (dst, da[:, cols])):
            ref[b, 0:256] = jnp.where(low, part, none)
            ref[b, 256:512] = jnp.where(low, none, part)

    def sub(z, yy, c):
        return kv.at[:, z, yy, c]

    def ag_copy_z(z, c, way):
        return remote(sub(z, y, c), sub(z, y, c), agz_s, agz_r.at[z, c], to_z[way])

    def ag_send_y(z, c):
        for k in (1, 3, 2):
            send(sub(z, y, c), sub(z, y, c), agy_s, agy_r.at[z], y_peer(after(y, k)), False)

    def ag_got_z(z, c):
        got(sub(z, y, c), agz_r.at[z, c])

    pltpu.make_async_copy(kv.at[:, zh, y, core], kv.at[:, zh, y, core], loc.at[1]).wait()

    @pl.when(core == 0)
    def _():
        ag_copy_z(zh, 0, 1).start()

    @pl.when(core == 1)
    def _():
        ag_copy_z(zh, 1, -1).start()

    got(sub(zh, y, other), sib_r.at[0])

    @pl.when(core == 1)
    def _():
        ag_copy_z(zh, 0, 1).start()

    @pl.when(core == 0)
    def _():
        ag_copy_z(zh, 1, -1).start()

    ag_copy_z(zh, 1, 1).start()
    ag_copy_z(zh, 0, -1).start()
    ag_send_y(zh, 0)
    ag_send_y(zh, 1)

    for c in local[5:]:
        c.wait()
    got(gb.at[pl.ds(pl.multiple_of(other * ROWS, ROWS), ROWS), :], sib_r.at[1])
    got(q2.at[pl.ds(pl.multiple_of(other * ROWS, ROWS), ROWS), :], sib_r.at[2])
    dat[...] = nt(w_v[...], gb[...]).astype(BF)
    da[...] = nt(gb[...], w_v[...]).astype(BF)
    prepare(0)
    prepare(1)

    ag_got_z(z3, 0)
    ag_copy_z(z3, 0, 1).start()
    ag_got_z(z1, 1)
    ag_copy_z(z1, 1, -1).start()
    ag_send_y(z3, 0)
    ag_send_y(z1, 1)
    ag_got_z(z3, 1)
    ag_send_y(z3, 1)
    ag_got_z(z1, 0)
    ag_send_y(z1, 0)
    for c in range(2):
        ag_got_z(z2, c)
        ag_send_y(z2, c)

    def keys_of(b, z):
        return kv[b, z, :, :, 0].reshape(256, 128)

    def values_of(b, z):
        return kv[b, z, :, :, 1].reshape(256, 128)

    def all_of(b, t):
        return kv[b, :, :, :, t].reshape(1024, 128)

    tops = [None, None]

    def scores(z):
        got(kv.at[:, z, 0:3], agy_r.at[z])
        for b in range(2):
            s = nn(keys_of(b, z), qbd[b])
            s_ref[b, z] = s
            m = jnp.max(s, axis=0, keepdims=True)
            tops[b] = m if tops[b] is None else jnp.maximum(tops[b], m)

    def forward(b):
        top = tops[b]
        total = None
        for r in range(4):
            e = jnp.exp2((s_ref[b, r] - top) * (SCALE * LOG2E))
            s_ref[b, r] = e
            m = jnp.sum(e, axis=0, keepdims=True)
            total = m if total is None else total + m
        inv = 1.0 / total
        for r in range(4):
            p = s_ref[b, r] * inv
            s_ref[b, r] = p
            pb_ref[b, r * 256 : r * 256 + 256] = p.astype(BF)
        a = tn(all_of(b, 1), pb_ref[b])
        at[b * 128 : b * 128 + 64, :] = a[0:64, 0:256].astype(BF)
        at[b * 128 + 64 : b * 128 + 128, :] = a[64:128, 256:512].astype(BF)

    def delta_of(b):
        cols = slice(b * 128, b * 128 + 128)
        prod = dat[cols, :].astype(F32) * at[cols, :].astype(F32)
        return jnp.concatenate(
            [jnp.sum(prod[0:64], axis=0, keepdims=True), jnp.sum(prod[64:128], axis=0, keepdims=True)], axis=1
        )

    def backward(b, z, delta):
        rows = pl.ds(pl.multiple_of(z * 256, 256), 256)
        dp = nn(values_of(b, z), dbd[b])
        ds = (s_ref[b, z] * (dp - delta)).astype(BF)
        ds_ref[b, rows] = ds
        dkv[b, z, :, :, 0] = (nn(ds, qst[b]) * SCALE).astype(BF).reshape(4, 2, LAT, 128)
        dkv[b, z, :, :, 1] = nn(pb_ref[b, rows], dst[b]).astype(BF).reshape(4, 2, LAT, 128)

    def query_part(b):
        a = tn(all_of(b, 0), ds_ref[b]) * SCALE
        for c in range(2):
            rows = slice(c * 128, c * 128 + 128)
            dqs[b, c] = jnp.concatenate([a[0:64, rows], a[64:128, 256 + c * 128 : 384 + c * 128]], axis=0).T
        dq_out[:, block_cols(core, b)] = dqs[b, core]
        send(dqs.at[b, other], dq_out.at[:, block_cols(core, b)], dq_s, dq_r, sib, False)

    def add(*parts):
        out = parts[0].astype(F32)
        for p in parts[1:]:
            out = out + p.astype(F32)
        return out

    def rs_y(z):
        for k in (1, 3, 2):
            peer = after(y, k)
            send(dkv.at[:, z, peer], ry.at[z, y], ry_s, ry_r.at[z], y_peer(peer), False)

    def y_sum(z):
        got(ry.at[z, 0:3], ry_r.at[z])
        red[:, z] = add(dkv[:, z, y], ry[z, y1], ry[z, y3], ry[z, y2]).astype(BF)

    def z_send(z, c, i, k):
        send(red.at[:, z, c], rz.at[i, k], rz_s.at[i, k], rz_r.at[i, k], to_z[1 - 2 * i])

    def z_got(i, k):
        got(rz.at[i, k], rz_r.at[i, k])

    def rs_z_far():
        y_sum(z2)
        z_send(z2, 0, 0, 0)
        z_send(z2, 1, 1, 0)

    def rs_z_near():
        y_sum(z1)
        z_send(z1, 1, 0, 1)
        y_sum(z3)
        z_send(z3, 0, 1, 1)

    def rs_z_last():
        z_got(0, 0)
        red[:, z1, 0] = add(red[:, z1, 0], rz[0, 0]).astype(BF)
        z_send(z1, 0, 0, 2)
        z_got(1, 0)
        red[:, z3, 1] = add(red[:, z3, 1], rz[1, 0]).astype(BF)
        z_send(z3, 1, 1, 2)

    def rs_end():
        z_got(0, 1)
        z_got(1, 1)
        z_got(0, 2)
        fin[0] = add(red[:, zh, 0], rz[0, 2], rz[1, 1])
        z_got(1, 2)
        fin[1] = add(red[:, zh, 1], rz[0, 1], rz[1, 2])
        for t, out in enumerate((dk_out, dv_out)):
            for b in range(2):
                send(fin.at[other, b, t], out.at[:, block_cols(core, b)], fin_s, fin_r.at[t], sib, False)
                out[:, block_cols(core, b)] = fin[core, b, t]

    def rs_got():
        for t, out in enumerate((dk_out, dv_out)):
            got(out.at[:, theirs], fin_r.at[t])
        got(dq_out.at[:, theirs], dq_r)

    def spread(at_me, make):
        @pl.loop(1, 16)
        def _(i):
            make(lax.rem(at_me + i, 16)).start()

    def w_start():
        wpart[...] = nn(at[...], gb[...]).astype(BF).reshape(16, 16, D)
        spread(plane, lambda i: remote(wpart.at[i], w_a.at[plane], a_s, a_r, plane_peer(i)))
        w_a[plane] = wpart[plane]

    def w_to_line():
        got(w_a.at[0:15], a_r)
        total = jnp.sum(w_a[...].astype(F32), axis=0)
        for p in range(4):
            w_b_src[p] = total[:, p * 128 : p * 128 + 128].astype(BF)
        spread(line, lambda i: remote(w_b_src.at[lax.rem(i, 4)], w_b.at[line], b_s, b_r, line_peer(i)))
        w_b[line] = w_b_src[zl]

    def w_to_near():
        got(w_b.at[0:15], b_r)
        w_c[zl] = (jnp.sum(w_b[...].astype(F32), axis=0) * (1.0 / SHAPES)).astype(BF)
        for k in (1, 3, 2):
            send(w_c.at[zl], w_c.at[zl], c_s, c_r, line_peer(zh * 4 + after(zl, k)), False)

    def w_back():
        got(w_c.at[0:3], c_r)
        for p in range(4):
            dw_out[core, plane, :, p * 128 : p * 128 + 128] = w_c[p]
        spread(plane, lambda i: remote(dw_out.at[core, plane], dw_out.at[core, plane], d_s, d_r, plane_peer(i)))

    def w_pair():
        got(dw_out.at[core, 0:15], d_r)
        send(dw_out.at[core], dw_out.at[core], e_s, e_r, sib)

    def back(z):
        for b in range(2):
            backward(b, z, deltas[b])
        rs_y(z)

    for z in (zh, z3, z1, z2):
        scores(z)
    forward(0)
    forward(1)
    w_start()
    deltas = (delta_of(0), delta_of(1))
    for z in (z2, z1, z3, zh):
        back(z)
    query_part(0)
    query_part(1)
    w_to_line()
    rs_z_far()
    rs_z_near()
    y_sum(zh)
    w_to_near()
    rs_z_last()
    w_back()
    rs_end()
    w_pair()
    rs_got()
    got(dw_out.at[other], e_r)

    sent(sub(zh, y, other), sib_s.at[0])
    sent(kv.at[:, 0, 0:3], agz_s)
    sent(kv.at[:, 0:3], agy_s)
    sent(dkv.at[:, 0:3], ry_s)
    sent(fin.at[0], fin_s)
    sent(dqs.at[:, 0], dq_s)
    sent(w_a.at[0:15], a_s)
    sent(w_b.at[0:15], b_s)
    sent(w_c.at[0:3], c_s)
    sent(dw_out.at[core, 0:15], d_s)
    for c in sends:
        c.wait_send()


def finish(dq, dk, dv, dw, dq_out, dk_out, dv_out, dw_out):
    dq_out[...] = dq[...]
    dk_out[...] = dk[...]
    dv_out[...] = dv[...]
    dw_out[...] = dw[...].astype(F32)


def shards(queries, keys, values, out_weight, out_grad):
    dma = pltpu.SemaphoreType.DMA
    vm = pltpu.VMEM
    one = pl.BlockSpec(memory_space=pltpu.VMEM)
    sizes = ((ROWS, D), (LAT, D), (LAT, D))
    dq, dk, dv, dw = pl.pallas_call(
        kernel,
        out_shape=[jax.ShapeDtypeStruct(i, F32) for i in sizes] + [jax.ShapeDtypeStruct((2, 16, 16, D), BF)],
        in_specs=[pl.BlockSpec(memory_space=pltpu.HBM)] * 5,
        out_specs=[one] * 4,
        scratch_shapes=[
            vm((2, 4, 4, 2, 2, LAT, 128), BF),
            vm((256, 256), BF),
            vm((256, D), BF),
            vm((ROWS, D), F32),
            vm((256, D), BF),
            vm((256, 256), BF),
            vm((256, 256), BF),
            vm((2, 4, 256, 512), F32),
            vm((2, 1024, 512), BF),
            vm((2, 1024, 512), BF),
            vm((256, 256), BF),
            vm((2, 128, 512), BF),
            vm((2, 128, 512), BF),
            vm((2, 512, 128), BF),
            vm((2, 512, 128), BF),
            vm((2, 4, 4, 2, 2, LAT, 128), BF),
            vm((4, 4, 2, 2, 2, LAT, 128), BF),
            vm((2, 3, 2, 2, LAT, 128), BF),
            vm((2, 4, 2, 2, LAT, 128), BF),
            vm((2, 2, 2, LAT, 128), F32),
            vm((2, 2, 128, 128), F32),
            vm((16, 16, D), BF),
            vm((16, 16, D), BF),
            vm((4, 16, 128), BF),
            vm((16, 16, 128), BF),
            vm((4, 16, 128), BF),
            dma((4,)), dma((3,)), dma((3,)),
            dma, dma((4, 2)), dma, dma((4,)),
            dma, dma((4,)), dma((2, 3)), dma((2, 3)),
            dma, dma((2,)), dma, dma,
            dma, dma, dma, dma, dma, dma, dma, dma, dma, dma,
        ],
        compiler_params=pltpu.CompilerParams(
            collective_id=0, has_side_effects=True, vmem_limit_bytes=58 * 1024 * 1024
        ),
        name="attend_back",
    )(queries[0], keys[0], values[0], out_weight, out_grad[0])
    dq, dk, dv, dw = pl.pallas_call(
        finish,
        out_shape=[jax.ShapeDtypeStruct(i, F32) for i in sizes + ((D, D),)],
        in_specs=[one] * 4,
        out_specs=[one] * 4,
        compiler_params=pltpu.CompilerParams(vmem_limit_bytes=58 * 1024 * 1024),
        name="finish",
    )(dq, dk, dv, dw.reshape(D, D))
    return (dq[None], dk[None], dv[None], dw)


def solution(mesh):
    part = P("shape", "query", None)
    return jax.shard_map(
        shards,
        mesh=mesh,
        in_specs=(part, part, part, P(), part),
        out_specs=(part, part, part, P()),
        check_vma=False,
    )
```

time: 84.8 us -> 69.6 us (0.82)
  Pallas kernels: 76.3 us -> 68.8 us
  local copies, waits for them, and re-layouts: 6.36 us -> 0 us
  other arithmetic: 1.14 us -> 0 us
    pallas_call x1 -> x2, Pallas kernels: 76.3 us -> 68.8 us  [the longest x1 66.5 us: shards(): pl.pallas_call(kernel, out_shape=[jax.ShapeDtypeStruct(i, F32) for i in s...]
    unnamed x13 -> x0, local copies, waits for them, and re-layouts: 6.36 us -> none
    convert_element_type x1 -> x0, other arithmetic: 1.14 us -> none  [shards(): return (dq[None], dk[None], dv[None], dw.reshape(D, D).astype(F32))]
where the time goes in v2:
time: 69.6 us; the launch traced here: 69.5 us
  Pallas kernels  68.8 us (99%)
    pallas_call x1, Pallas kernels, shards(): pl.pallas_call(kernel, out_shape=[jax.ShapeDtypeStruct(i, F32) for i in s...  66.5 us
    pallas_call x1, Pallas kernels, shards(): pl.pallas_call(finish, out_shape=[jax.ShapeDtypeStruct(i, F32) for i in s...  2.3 us

profile of v2, /device:TPU:1, one launch (start us, length us, event | category | flops | bytes accessed | tf_op | source)
XLA Modules:
  0.0 69.5 jit_solution(2287461379147531183)
XLA Ops:
  0.6 66.5 %attend_back.1 = (f32[128,512]{1,0:T(8,128)}, f32[32,512]{1,0:T(8,128)}, f32[32,512]{1,0:T(8,128)}, bf16[2,16,16,512]{3,2,1,0:T(8,128)(2,1)}) custom-call(bf16[128,512]{1,0:T(8,128)(2,1)} %bitcast.10, bf16[32,512]{1,0:T(8,128)(2,1)} %bitcast.11, bf16[32,512]{1,0:T(8,128)(2,1)} %bitcast.12, bf16[512,512]{1,0:T(8,128)(2,1)} %w_hbm.1, f32[128,512]{1,0:T(8,128)} %bitcast.9), custom_call_target="tpu_custom_call" | custom-call | tf_op jit(solution)/shard_map/attend_back/pallas_call | solution.py:414
  67.2 2.3 %finish.1 = (f32[128,512]{1,0:T(8,128)}, f32[32,512]{1,0:T(8,128)}, f32[32,512]{1,0:T(8,128)}, f32[512,512]{1,0:T(8,128)}) custom-call(f32[128,512]{1,0:T(8,128)} %get-tuple-element.12.dq, f32[32,512]{1,0:T(8,128)} %get-tuple-element.13.dk, f32[32,512]{1,0:T(8,128)} %get-tuple-element.14.dv, bf16[512,512]{1,0:T(8,128)(2,1)} %bitcast.8), custom_call_target="tpu_custom_call" | custom-call | tf_op jit(solution)/shard_map/finish/pallas_call | solution.py:457

commit v3 on v2

--- a/solution.py
+++ b/solution.py
@@ -18,6 +18,9 @@
 SHAPES = 16
 SCALE = 1.0 / math.sqrt(64)
 LOG2E = 1.4426950408889634
+RING = (2, 1, 3)
+PLANE = ((2, 2), (2, 1), (2, 3), (1, 2), (3, 2), (2, 0), (0, 2), (1, 1), (1, 3), (3, 1), (3, 3), (1, 0), (3, 0), (0, 1), (0, 3))
+LINE = (8, 7, 9, 6, 10, 5, 11, 4, 12, 3, 13, 2, 14, 1, 15)
 
 
 def nt(a, b):
@@ -35,8 +38,8 @@
 def kernel(
     q_hbm, k_hbm, v_hbm, w_hbm, g_hbm,
     dq_out, dk_out, dv_out, dw_out,
-    kv, q2, gb, gst, w_v, dat, da, s_ref, pb_ref, ds_ref, at, qbd, dbd, qst, dst,
-    dkv, ry, rz, red, fin, dqs, wpart, w_a, w_b_src, w_b, w_c,
+    kv, q2, gb, gst, w_v, dat, da, s_ref, ap, ds_ref, at, qbd, dbd, qst, dst,
+    dkv, ry, rz, red, fin, dqs, wpart, w_a, w_b_src, w_b, w_c, w_d,
     loc, sib_s, sib_r, agz_s, agz_r, agy_s, agy_r, ry_s, ry_r, rz_s, rz_r, fin_s, fin_r, dq_s, dq_r,
     a_s, a_r, b_s, b_r, c_s, c_r, d_s, d_r, e_s, e_r,
 ):
@@ -53,20 +56,23 @@
     sib = (shape_at, query_at + 1 - 2 * core)
     to_z = {1: (shape_at, z1 * 8 + y * 2 + core), -1: (shape_at, z3 * 8 + y * 2 + core)}
     to_y = {1: (shape_at, zh * 8 + y1 * 2 + core), -1: (shape_at, zh * 8 + y3 * 2 + core)}
+    def after(i, k):
+        return lax.rem(i + k, 4)
+
     line = zh * 4 + zl
     plane = x * 4 + y
 
     def y_peer(i):
         return (shape_at, zh * 8 + i * 2 + core)
 
-    def plane_peer(i):
-        return (zl * 4 + lax.div(i, 4), zh * 8 + lax.rem(i, 4) * 2 + core)
+    def plane_at(d):
+        return after(x, d[0]) * 4 + after(y, d[1])
+
+    def plane_peer(d):
+        return (zl * 4 + after(x, d[0]), zh * 8 + after(y, d[1]) * 2 + core)
 
     def line_peer(i):
         return (lax.rem(i, 4) * 4 + x, lax.div(i, 4) * 8 + y * 2 + core)
-
-    def after(i, k):
-        return lax.rem(i + k, 4)
 
     barrier = pltpu.get_barrier_semaphore()
 
@@ -78,10 +84,8 @@
     for k in (1, 2, 3):
         greet(line_peer(zh * 4 + after(zl, k)))
 
-    @pl.loop(1, 16)
-    def _(i):
-        greet(plane_peer(lax.rem(plane + i, 16)))
-
+    for d in PLANE:
+        greet(plane_peer(d))
     greet(sib)
 
     mine = pl.ds(pl.multiple_of(core * HALF, HALF), HALF)
@@ -105,6 +109,12 @@
     gb[my_rows, :] = gst[...].astype(BF)
 
     sends = []
+    kept = []
+
+    def keep(src, dst):
+        c = pltpu.make_async_copy(src, dst, loc.at[4 + len(kept)])
+        c.start()
+        kept.append(c)
 
     def remote(src, dst, ss, rs, dev):
         return pltpu.make_async_remote_copy(
@@ -150,40 +160,29 @@
     def sub(z, yy, c):
         return kv.at[:, z, yy, c]
 
-    def ag_copy_z(z, c, way):
-        return remote(sub(z, y, c), sub(z, y, c), agz_s, agz_r.at[z, c], to_z[way])
-
-    def ag_send_y(z, c):
-        for k in (1, 3, 2):
-            send(sub(z, y, c), sub(z, y, c), agy_s, agy_r.at[z], y_peer(after(y, k)), False)
-
-    def ag_got_z(z, c):
-        got(sub(z, y, c), agz_r.at[z, c])
+    def ag_z(ref, way, sem):
+        return remote(ref, ref, agz_s, agz_r.at[sem], to_z[way])
+
+    def ag_send_y(ref, sem):
+        for k in RING:
+            send(ref, ref, agy_s, agy_r.at[sem], y_peer(after(y, k)), False)
+
+    def half(z, c, b):
+        return kv.at[b, z, y, c]
+
+    def ag_ahead(c):
+        for b in range(2):
+            ag_z(half(zh, c, b), 1 - 2 * c, 3 * c + b).start()
 
     pltpu.make_async_copy(kv.at[:, zh, y, core], kv.at[:, zh, y, core], loc.at[1]).wait()
-
-    @pl.when(core == 0)
-    def _():
-        ag_copy_z(zh, 0, 1).start()
-
-    @pl.when(core == 1)
-    def _():
-        ag_copy_z(zh, 1, -1).start()
-
+    for c in range(2):
+        pl.when(core == c)(lambda c=c: ag_ahead(c))
     got(sub(zh, y, other), sib_r.at[0])
-
-    @pl.when(core == 1)
-    def _():
-        ag_copy_z(zh, 0, 1).start()
-
-    @pl.when(core == 0)
-    def _():
-        ag_copy_z(zh, 1, -1).start()
-
-    ag_copy_z(zh, 1, 1).start()
-    ag_copy_z(zh, 0, -1).start()
-    ag_send_y(zh, 0)
-    ag_send_y(zh, 1)
+    for c in range(2):
+        pl.when(core != c)(lambda c=c: ag_ahead(c))
+    ag_z(sub(zh, y, 1), 1, 2).start()
+    ag_z(sub(zh, y, 0), -1, 5).start()
+    ag_send_y(kv.at[:, zh, y], 0)
 
     for c in local[5:]:
         c.wait()
@@ -194,19 +193,18 @@
     prepare(0)
     prepare(1)
 
-    ag_got_z(z3, 0)
-    ag_copy_z(z3, 0, 1).start()
-    ag_got_z(z1, 1)
-    ag_copy_z(z1, 1, -1).start()
-    ag_send_y(z3, 0)
-    ag_send_y(z1, 1)
-    ag_got_z(z3, 1)
-    ag_send_y(z3, 1)
-    ag_got_z(z1, 0)
-    ag_send_y(z1, 0)
-    for c in range(2):
-        ag_got_z(z2, c)
-        ag_send_y(z2, c)
+    for b in range(2):
+        for z, c, way in ((z3, 0, 1), (z1, 1, -1)):
+            got(half(z, c, b), agz_r.at[3 * c + b])
+            ag_z(half(z, c, b), way, 6 + 2 * c + b).start()
+            ag_send_y(half(z, c, b), 1 + c)
+    for z, c in ((z3, 1), (z1, 0)):
+        got(sub(z, y, c), agz_r.at[2 + 3 * (1 - c)])
+        ag_send_y(sub(z, y, c), 2 - c)
+    for b in range(2):
+        for c in range(2):
+            got(half(z2, c, b), agz_r.at[6 + 2 * c + b])
+        ag_send_y(kv.at[b, z2, y], 3 + b)
 
     def keys_of(b, z):
         return kv[b, z, :, :, 0].reshape(256, 128)
@@ -217,32 +215,37 @@
     def all_of(b, t):
         return kv[b, :, :, :, t].reshape(1024, 128)
 
-    tops = [None, None]
-
-    def scores(z):
-        got(kv.at[:, z, 0:3], agy_r.at[z])
-        for b in range(2):
-            s = nn(keys_of(b, z), qbd[b])
-            s_ref[b, z] = s
-            m = jnp.max(s, axis=0, keepdims=True)
-            tops[b] = m if tops[b] is None else jnp.maximum(tops[b], m)
-
-    def forward(b):
-        top = tops[b]
-        total = None
-        for r in range(4):
-            e = jnp.exp2((s_ref[b, r] - top) * (SCALE * LOG2E))
-            s_ref[b, r] = e
-            m = jnp.sum(e, axis=0, keepdims=True)
-            total = m if total is None else total + m
+    order = (zh, z3, z1, z2)
+    tops, totals, gains = ([[None] * 2 for _ in range(4)] for _ in range(3))
+
+    def score(i, b):
+        sc = nn(keys_of(b, order[i]), qbd[b])
+        top = jnp.max(sc, axis=0, keepdims=True)
+        e = jnp.exp2((sc - top) * (SCALE * LOG2E))
+        s_ref[b, i] = e
+        tops[i][b] = top
+        totals[i][b] = jnp.sum(e, axis=0, keepdims=True)
+        a = tn(values_of(b, order[i]), e.astype(BF))
+        ap[b, i, 0:64, :] = a[0:64, 0:256]
+        ap[b, i, 64:128, :] = a[64:128, 256:512]
+
+    def combine(b):
+        top = tops[0][b]
+        for i in range(1, 4):
+            top = jnp.maximum(top, tops[i][b])
+        f = [jnp.exp2((tops[i][b] - top) * (SCALE * LOG2E)) for i in range(4)]
+        total = f[0] * totals[0][b]
+        for i in range(1, 4):
+            total = total + f[i] * totals[i][b]
         inv = 1.0 / total
-        for r in range(4):
-            p = s_ref[b, r] * inv
-            s_ref[b, r] = p
-            pb_ref[b, r * 256 : r * 256 + 256] = p.astype(BF)
-        a = tn(all_of(b, 1), pb_ref[b])
-        at[b * 128 : b * 128 + 64, :] = a[0:64, 0:256].astype(BF)
-        at[b * 128 + 64 : b * 128 + 128, :] = a[64:128, 256:512].astype(BF)
+        for i in range(4):
+            gains[i][b] = f[i] * inv
+        for h in range(2):
+            a = None
+            for i in range(4):
+                part = ap[b, i, h * 64 : h * 64 + 64, :] * gains[i][b][:, h * 256 : h * 256 + 256]
+                a = part if a is None else a + part
+            at[b * 128 + h * 64 : b * 128 + h * 64 + 64, :] = a.astype(BF)
 
     def delta_of(b):
         cols = slice(b * 128, b * 128 + 128)
@@ -251,20 +254,22 @@
             [jnp.sum(prod[0:64], axis=0, keepdims=True), jnp.sum(prod[64:128], axis=0, keepdims=True)], axis=1
         )
 
-    def backward(b, z, delta):
+    def backward(i, b, delta):
+        z = order[i]
         rows = pl.ds(pl.multiple_of(z * 256, 256), 256)
+        p = s_ref[b, i] * gains[i][b]
         dp = nn(values_of(b, z), dbd[b])
-        ds = (s_ref[b, z] * (dp - delta)).astype(BF)
+        ds = (p * (dp - delta)).astype(BF)
         ds_ref[b, rows] = ds
         dkv[b, z, :, :, 0] = (nn(ds, qst[b]) * SCALE).astype(BF).reshape(4, 2, LAT, 128)
-        dkv[b, z, :, :, 1] = nn(pb_ref[b, rows], dst[b]).astype(BF).reshape(4, 2, LAT, 128)
+        dkv[b, z, :, :, 1] = nn(p.astype(BF), dst[b]).astype(BF).reshape(4, 2, LAT, 128)
 
     def query_part(b):
         a = tn(all_of(b, 0), ds_ref[b]) * SCALE
         for c in range(2):
             rows = slice(c * 128, c * 128 + 128)
             dqs[b, c] = jnp.concatenate([a[0:64, rows], a[64:128, 256 + c * 128 : 384 + c * 128]], axis=0).T
-        dq_out[:, block_cols(core, b)] = dqs[b, core]
+        keep(dqs.at[b, core], dq_out.at[:, block_cols(core, b)])
         send(dqs.at[b, other], dq_out.at[:, block_cols(core, b)], dq_s, dq_r, sib, False)
 
     def add(*parts):
@@ -274,7 +279,7 @@
         return out
 
     def rs_y(z):
-        for k in (1, 3, 2):
+        for k in RING:
             peer = after(y, k)
             send(dkv.at[:, z, peer], ry.at[z, y], ry_s, ry_r.at[z], y_peer(peer), False)
 
@@ -317,21 +322,17 @@
         for t, out in enumerate((dk_out, dv_out)):
             for b in range(2):
                 send(fin.at[other, b, t], out.at[:, block_cols(core, b)], fin_s, fin_r.at[t], sib, False)
-                out[:, block_cols(core, b)] = fin[core, b, t]
+                keep(fin.at[core, b, t], out.at[:, block_cols(core, b)])
 
     def rs_got():
         for t, out in enumerate((dk_out, dv_out)):
             got(out.at[:, theirs], fin_r.at[t])
         got(dq_out.at[:, theirs], dq_r)
 
-    def spread(at_me, make):
-        @pl.loop(1, 16)
-        def _(i):
-            make(lax.rem(at_me + i, 16)).start()
-
     def w_start():
         wpart[...] = nn(at[...], gb[...]).astype(BF).reshape(16, 16, D)
-        spread(plane, lambda i: remote(wpart.at[i], w_a.at[plane], a_s, a_r, plane_peer(i)))
+        for d in PLANE:
+            send(wpart.at[plane_at(d)], w_a.at[plane], a_s, a_r, plane_peer(d), False)
         w_a[plane] = wpart[plane]
 
     def w_to_line():
@@ -339,7 +340,9 @@
         total = jnp.sum(w_a[...].astype(F32), axis=0)
         for p in range(4):
             w_b_src[p] = total[:, p * 128 : p * 128 + 128].astype(BF)
-        spread(line, lambda i: remote(w_b_src.at[lax.rem(i, 4)], w_b.at[line], b_s, b_r, line_peer(i)))
+        for k in LINE:
+            peer = lax.rem(line + k, 16)
+            send(w_b_src.at[lax.rem(peer, 4)], w_b.at[line], b_s, b_r, line_peer(peer), False)
         w_b[line] = w_b_src[zl]
 
     def w_to_near():
@@ -351,26 +354,32 @@
     def w_back():
         got(w_c.at[0:3], c_r)
         for p in range(4):
-            dw_out[core, plane, :, p * 128 : p * 128 + 128] = w_c[p]
-        spread(plane, lambda i: remote(dw_out.at[core, plane], dw_out.at[core, plane], d_s, d_r, plane_peer(i)))
+            w_d[plane, :, p * 128 : p * 128 + 128] = w_c[p]
+        for d in PLANE:
+            send(w_d.at[plane], w_d.at[plane], d_s, d_r, plane_peer(d), False)
 
     def w_pair():
-        got(dw_out.at[core, 0:15], d_r)
-        send(dw_out.at[core], dw_out.at[core], e_s, e_r, sib)
-
-    def back(z):
+        got(w_d.at[0:15], d_r)
+        send(w_d, dw_out.at[core], e_s, e_r, sib)
+        keep(w_d, dw_out.at[core])
+
+    def back(i):
         for b in range(2):
-            backward(b, z, deltas[b])
-        rs_y(z)
-
-    for z in (zh, z3, z1, z2):
-        scores(z)
-    forward(0)
-    forward(1)
+            backward(i, b, deltas[b])
+        rs_y(order[i])
+
+    for i in range(3):
+        got(kv.at[:, order[i], 0:3], agy_r.at[i])
+        score(i, 0)
+        score(i, 1)
+    for b in range(2):
+        got(kv.at[b, z2, 0:3], agy_r.at[3 + b])
+        score(3, b)
+        combine(b)
     w_start()
     deltas = (delta_of(0), delta_of(1))
-    for z in (z2, z1, z3, zh):
-        back(z)
+    for i in (3, 2, 1, 0):
+        back(i)
     query_part(0)
     query_part(1)
     w_to_line()
@@ -394,27 +403,39 @@
     sent(w_a.at[0:15], a_s)
     sent(w_b.at[0:15], b_s)
     sent(w_c.at[0:3], c_s)
-    sent(dw_out.at[core, 0:15], d_s)
+    sent(w_d.at[0:15], d_s)
+    for c in kept:
+        c.wait()
     for c in sends:
         c.wait_send()
 
 
-def finish(dq, dk, dv, dw, dq_out, dk_out, dv_out, dw_out):
-    dq_out[...] = dq[...]
-    dk_out[...] = dk[...]
-    dv_out[...] = dv[...]
-    dw_out[...] = dw[...].astype(F32)
+def finish(dq, dk, dv, dw, dq_out, dk_out, dv_out, dw_out, vq, vk, vv, half, full, sem):
+    rest = ((dq, vq, dq_out), (dk, vk, dk_out), (dv, vv, dv_out))
+    loads = [pltpu.make_async_copy(dw.at[pl.ds(i * 128, 128)], half.at[i], sem.at[i]) for i in range(4)]
+    loads += [pltpu.make_async_copy(src, mid, sem.at[4 + i]) for i, (src, mid, _) in enumerate(rest)]
+    stores = [pltpu.make_async_copy(full.at[i], dw_out.at[pl.ds(i * 128, 128)], sem.at[7 + i]) for i in range(4)]
+    stores += [pltpu.make_async_copy(mid, dst, sem.at[11 + i]) for i, (_, mid, dst) in enumerate(rest)]
+    for c in loads:
+        c.start()
+    for i in range(7):
+        loads[i].wait()
+        if i < 4:
+            full[i] = half[i].astype(F32)
+        stores[i].start()
+    for c in stores:
+        c.wait()
 
 
 def shards(queries, keys, values, out_weight, out_grad):
     dma = pltpu.SemaphoreType.DMA
     vm = pltpu.VMEM
-    one = pl.BlockSpec(memory_space=pltpu.VMEM)
+    one = pl.BlockSpec(memory_space=pltpu.HBM)
     sizes = ((ROWS, D), (LAT, D), (LAT, D))
     dq, dk, dv, dw = pl.pallas_call(
         kernel,
         out_shape=[jax.ShapeDtypeStruct(i, F32) for i in sizes] + [jax.ShapeDtypeStruct((2, 16, 16, D), BF)],
-        in_specs=[pl.BlockSpec(memory_space=pltpu.HBM)] * 5,
+        in_specs=[one] * 5,
         out_specs=[one] * 4,
         scratch_shapes=[
             vm((2, 4, 4, 2, 2, LAT, 128), BF),
@@ -425,7 +446,7 @@
             vm((256, 256), BF),
             vm((256, 256), BF),
             vm((2, 4, 256, 512), F32),
-            vm((2, 1024, 512), BF),
+            vm((2, 4, 128, 256), F32),
             vm((2, 1024, 512), BF),
             vm((256, 256), BF),
             vm((2, 128, 512), BF),
@@ -443,8 +464,9 @@
             vm((4, 16, 128), BF),
             vm((16, 16, 128), BF),
             vm((4, 16, 128), BF),
-            dma((4,)), dma((3,)), dma((3,)),
-            dma, dma((4, 2)), dma, dma((4,)),
+            vm((16, 16, D), BF),
+            dma((11,)), dma((3,)), dma((3,)),
+            dma, dma((10,)), dma, dma((5,)),
             dma, dma((4,)), dma((2, 3)), dma((2, 3)),
             dma, dma((2,)), dma, dma,
             dma, dma, dma, dma, dma, dma, dma, dma, dma, dma,
@@ -459,6 +481,7 @@
         out_shape=[jax.ShapeDtypeStruct(i, F32) for i in sizes + ((D, D),)],
         in_specs=[one] * 4,
         out_specs=[one] * 4,
+        scratch_shapes=[vm(i, F32) for i in sizes] + [vm((4, 128, D), BF), vm((4, 128, D), F32), dma((14,))],
         compiler_params=pltpu.CompilerParams(vmem_limit_bytes=58 * 1024 * 1024),
         name="finish",
     )(dq, dk, dv, dw.reshape(D, D))

time: 69.6 us -> 66.1 us (0.950)
  Pallas kernels: 68.8 us -> 65.3 us
    pallas_call x1, Pallas kernels: 66.5 us -> 63.2 us  [shards(): pl.pallas_call(kernel, out_shape=[jax.ShapeDtypeStruct(i, F32) for i in s...]
where the time goes in v3:
time: 66.1 us; the launch traced here: 66 us
  Pallas kernels  65.3 us (99%)
    pallas_call x1, Pallas kernels, shards(): pl.pallas_call(kernel, out_shape=[jax.ShapeDtypeStruct(i, F32) for i in s...  63.2 us
    pallas_call x1, Pallas kernels, shards(): pl.pallas_call(finish, out_shape=[jax.ShapeDtypeStruct(i, F32) for i in s...  2.13 us

profile of v3, /device:TPU:1, one launch (start us, length us, event | category | flops | bytes accessed | tf_op | source)
XLA Modules:
  0.0 66.0 jit_solution(5148930317983900780)
XLA Ops:
  0.6 63.2 %attend_back.1 = (f32[128,512]{1,0:T(8,128)}, f32[32,512]{1,0:T(8,128)}, f32[32,512]{1,0:T(8,128)}, bf16[2,16,16,512]{3,2,1,0:T(8,128)(2,1)}) custom-call(bf16[128,512]{1,0:T(8,128)(2,1)} %bitcast.10, bf16[32,512]{1,0:T(8,128)(2,1)} %bitcast.11, bf16[32,512]{1,0:T(8,128)(2,1)} %bitcast.12, bf16[512,512]{1,0:T(8,128)(2,1)} %w_hbm.1, f32[128,512]{1,0:T(8,128)} %bitcast.9), custom_call_target="tpu_custom_call" | custom-call | tf_op jit(solution)/shard_map/attend_back/pallas_call | solution.py:435
  63.8 2.1 %finish.1 = (f32[128,512]{1,0:T(8,128)}, f32[32,512]{1,0:T(8,128)}, f32[32,512]{1,0:T(8,128)}, f32[512,512]{1,0:T(8,128)}) custom-call(f32[128,512]{1,0:T(8,128)} %get-tuple-element.12.dq, f32[32,512]{1,0:T(8,128)} %get-tuple-element.13.dk, f32[32,512]{1,0:T(8,128)} %get-tuple-element.14.dv, bf16[512,512]{1,0:T(8,128)(2,1)} %bitcast.8), custom_call_target="tpu_custom_call" | custom-call | tf_op jit(solution)/shard_map/finish/pallas_call | solution.py:479

commit v4 on v3

--- a/solution.py
+++ b/solution.py
@@ -278,46 +278,46 @@
             out = out + p.astype(F32)
         return out
 
-    def rs_y(z):
+    def rs_y(i):
         for k in RING:
             peer = after(y, k)
-            send(dkv.at[:, z, peer], ry.at[z, y], ry_s, ry_r.at[z], y_peer(peer), False)
-
-    def y_sum(z):
-        got(ry.at[z, 0:3], ry_r.at[z])
-        red[:, z] = add(dkv[:, z, y], ry[z, y1], ry[z, y3], ry[z, y2]).astype(BF)
-
-    def z_send(z, c, i, k):
-        send(red.at[:, z, c], rz.at[i, k], rz_s.at[i, k], rz_r.at[i, k], to_z[1 - 2 * i])
-
-    def z_got(i, k):
-        got(rz.at[i, k], rz_r.at[i, k])
-
-    def rs_z_far():
-        y_sum(z2)
-        z_send(z2, 0, 0, 0)
-        z_send(z2, 1, 1, 0)
+            send(dkv.at[:, order[i], peer], ry.at[i, y], ry_s, ry_r.at[i], y_peer(peer), False)
+
+    def rs_y_far(b):
+        for k in RING:
+            peer = after(y, k)
+            send(dkv.at[b, z2, peer], ry.at[3, y, b], ry_s, ry_r.at[3 + b], y_peer(peer), False)
+
+    def y_sum(i):
+        got(ry.at[i, 0:3], ry_r.at[i])
+        red[:, order[i]] = add(dkv[:, order[i], y], ry[i, y1], ry[i, y3], ry[i, y2]).astype(BF)
+
+    def z_send(src, dst, i, k):
+        send(src, dst, rz_s.at[i, k], rz_r.at[i, k], to_z[1 - 2 * i])
+
+    def rs_z_far(b):
+        got(ry.at[3, 0:3, b], ry_r.at[3 + b])
+        red[b, z2] = add(dkv[b, z2, y], ry[3, y1, b], ry[3, y3, b], ry[3, y2, b]).astype(BF)
+        for c in range(2):
+            z_send(red.at[b, z2, c], rz.at[c, 0, b], c, b)
 
     def rs_z_near():
-        y_sum(z1)
-        z_send(z1, 1, 0, 1)
-        y_sum(z3)
-        z_send(z3, 0, 1, 1)
-
-    def rs_z_last():
-        z_got(0, 0)
-        red[:, z1, 0] = add(red[:, z1, 0], rz[0, 0]).astype(BF)
-        z_send(z1, 0, 0, 2)
-        z_got(1, 0)
-        red[:, z3, 1] = add(red[:, z3, 1], rz[1, 0]).astype(BF)
-        z_send(z3, 1, 1, 2)
+        for i, z, c in ((2, z1, 0), (1, z3, 1)):
+            y_sum(i)
+            z_send(red.at[:, z, 1 - c], rz.at[c, 1], c, 2)
+
+    def rs_z_last(b):
+        for c, z in enumerate((z1, z3)):
+            got(rz.at[c, 0, b], rz_r.at[c, b])
+            red[b, z, c] = add(red[b, z, c], rz[c, 0, b]).astype(BF)
+            z_send(red.at[b, z, c], rz.at[c, 2, b], c, 3 + b)
 
     def rs_end():
-        z_got(0, 1)
-        z_got(1, 1)
-        z_got(0, 2)
+        for c in range(2):
+            got(rz.at[c, 1], rz_r.at[c, 2])
+            for b in range(2):
+                got(rz.at[c, 2, b], rz_r.at[c, 3 + b])
         fin[0] = add(red[:, zh, 0], rz[0, 2], rz[1, 1])
-        z_got(1, 2)
         fin[1] = add(red[:, zh, 1], rz[0, 1], rz[1, 2])
         for t, out in enumerate((dk_out, dv_out)):
             for b in range(2):
@@ -329,13 +329,21 @@
             got(out.at[:, theirs], fin_r.at[t])
         got(dq_out.at[:, theirs], dq_r)
 
-    def w_start():
-        wpart[...] = nn(at[...], gb[...]).astype(BF).reshape(16, 16, D)
-        for d in PLANE:
-            send(wpart.at[plane_at(d)], w_a.at[plane], a_s, a_r, plane_peer(d), False)
+    def w_start(b):
+        rows = slice(b * 128, b * 128 + 128)
+        wpart[b * 8 : b * 8 + 8] = nn(at[rows, :], gb[...]).astype(BF).reshape(8, 16, D)
+        for k in (2, 1, 3, 0):
+            for px in (2 * b, 2 * b + 1):
+                peer = px * 4 + after(y, k)
+                dev = (zl * 4 + px, zh * 8 + after(y, k) * 2 + core)
+                c = remote(wpart.at[peer], w_a.at[plane], a_s, a_r, dev)
+                if k == 0:
+                    pl.when(px != x)(c.start)
+                else:
+                    c.start()
+
+    def w_to_line():
         w_a[plane] = wpart[plane]
-
-    def w_to_line():
         got(w_a.at[0:15], a_r)
         total = jnp.sum(w_a[...].astype(F32), axis=0)
         for p in range(4):
@@ -348,8 +356,8 @@
     def w_to_near():
         got(w_b.at[0:15], b_r)
         w_c[zl] = (jnp.sum(w_b[...].astype(F32), axis=0) * (1.0 / SHAPES)).astype(BF)
-        for k in (1, 3, 2):
-            send(w_c.at[zl], w_c.at[zl], c_s, c_r, line_peer(zh * 4 + after(zl, k)), False)
+        for k in (2, 1, 15):
+            send(w_c.at[zl], w_c.at[zl], c_s, c_r, line_peer(lax.rem(line + k, 16)), False)
 
     def w_back():
         got(w_c.at[0:3], c_r)
@@ -366,7 +374,7 @@
     def back(i):
         for b in range(2):
             backward(i, b, deltas[b])
-        rs_y(order[i])
+        rs_y(i)
 
     for i in range(3):
         got(kv.at[:, order[i], 0:3], agy_r.at[i])
@@ -376,21 +384,26 @@
         got(kv.at[b, z2, 0:3], agy_r.at[3 + b])
         score(3, b)
         combine(b)
-    w_start()
+        w_start(b)
     deltas = (delta_of(0), delta_of(1))
-    for i in (3, 2, 1, 0):
+    for b in range(2):
+        backward(3, b, deltas[b])
+        rs_y_far(b)
+    for i in (2, 1, 0):
         back(i)
     query_part(0)
     query_part(1)
     w_to_line()
-    rs_z_far()
+    rs_z_far(0)
+    rs_z_far(1)
+    w_to_near()
     rs_z_near()
-    y_sum(zh)
-    w_to_near()
-    rs_z_last()
+    y_sum(0)
+    rs_z_last(0)
+    rs_z_last(1)
     w_back()
+    w_pair()
     rs_end()
-    w_pair()
     rs_got()
     got(dw_out.at[other], e_r)
 
@@ -467,7 +480,7 @@
             vm((16, 16, D), BF),
             dma((11,)), dma((3,)), dma((3,)),
             dma, dma((10,)), dma, dma((5,)),
-            dma, dma((4,)), dma((2, 3)), dma((2, 3)),
+            dma, dma((5,)), dma((2, 5)), dma((2, 5)),
             dma, dma((2,)), dma, dma,
             dma, dma, dma, dma, dma, dma, dma, dma, dma, dma,
         ],

time: 66.1 us -> 61.7 us (0.933)
  Pallas kernels: 65.3 us -> 60.9 us
    pallas_call x1, Pallas kernels: 63.2 us -> 58.8 us  [shards(): pl.pallas_call(kernel, out_shape=[jax.ShapeDtypeStruct(i, F32) for i in s...]
where the time goes in v4:
time: 61.7 us; the launch traced here: 61.6 us
  Pallas kernels  60.9 us (99%)
  between operations  0.64 us (1%)
    pallas_call x1, Pallas kernels, shards(): pl.pallas_call(kernel, out_shape=[jax.ShapeDtypeStruct(i, F32) for i in s...  58.8 us
    pallas_call x1, Pallas kernels, shards(): pl.pallas_call(finish, out_shape=[jax.ShapeDtypeStruct(i, F32) for i in s...  2.13 us

profile of v4, /device:TPU:1, one launch (start us, length us, event | category | flops | bytes accessed | tf_op | source)
XLA Modules:
  0.0 61.6 jit_solution(17768272432861537922)
XLA Ops:
  0.6 58.8 %attend_back.1 = (f32[128,512]{1,0:T(8,128)}, f32[32,512]{1,0:T(8,128)}, f32[32,512]{1,0:T(8,128)}, bf16[2,16,16,512]{3,2,1,0:T(8,128)(2,1)}) custom-call(bf16[128,512]{1,0:T(8,128)(2,1)} %bitcast.10, bf16[32,512]{1,0:T(8,128)(2,1)} %bitcast.11, bf16[32,512]{1,0:T(8,128)(2,1)} %bitcast.12, bf16[512,512]{1,0:T(8,128)(2,1)} %w_hbm.1, f32[128,512]{1,0:T(8,128)} %bitcast.9), custom_call_target="tpu_custom_call" | custom-call | tf_op jit(solution)/shard_map/attend_back/pallas_call | solution.py:448
  59.5 2.1 %finish.1 = (f32[128,512]{1,0:T(8,128)}, f32[32,512]{1,0:T(8,128)}, f32[32,512]{1,0:T(8,128)}, f32[512,512]{1,0:T(8,128)}) custom-call(f32[128,512]{1,0:T(8,128)} %get-tuple-element.12.dq, f32[32,512]{1,0:T(8,128)} %get-tuple-element.13.dk, f32[32,512]{1,0:T(8,128)} %get-tuple-element.14.dv, bf16[512,512]{1,0:T(8,128)(2,1)} %bitcast.8), custom_call_target="tpu_custom_call" | custom-call | tf_op jit(solution)/shard_map/finish/pallas_call | solution.py:492

commit v5 on v4

--- a/solution.py
+++ b/solution.py
@@ -39,8 +39,8 @@
     q_hbm, k_hbm, v_hbm, w_hbm, g_hbm,
     dq_out, dk_out, dv_out, dw_out,
     kv, q2, gb, gst, w_v, dat, da, s_ref, ap, ds_ref, at, qbd, dbd, qst, dst,
-    dkv, ry, rz, red, fin, dqs, wpart, w_a, w_b_src, w_b, w_c, w_d,
-    loc, sib_s, sib_r, agz_s, agz_r, agy_s, agy_r, ry_s, ry_r, rz_s, rz_r, fin_s, fin_r, dq_s, dq_r,
+    dkv, ry, rz, rzf, own, red, fin, dqs, wpart, w_a, w_b_src, w_b, w_c, w_d,
+    loc, sib_s, sib_r, agz_s, agz_r, agy_s, agy_r, ry_s, ry_r, rz_s, rz_r, rf_r, fin_s, fin_r, dq_s, dq_r,
     a_s, a_r, b_s, b_r, c_s, c_r, d_s, d_r, e_s, e_r,
 ):
     shape_at = lax.axis_index("shape")
@@ -55,6 +55,9 @@
     z1, z2, z3 = [lax.rem(zh + i, 4) for i in (1, 2, 3)]
     sib = (shape_at, query_at + 1 - 2 * core)
     to_z = {1: (shape_at, z1 * 8 + y * 2 + core), -1: (shape_at, z3 * 8 + y * 2 + core)}
+    def to_z_core(way, c):
+        return (shape_at, (z1 if way == 1 else z3) * 8 + y * 2 + c)
+
     to_y = {1: (shape_at, zh * 8 + y1 * 2 + core), -1: (shape_at, zh * 8 + y3 * 2 + core)}
     def after(i, k):
         return lax.rem(i + k, 4)
@@ -295,6 +298,9 @@
     def z_send(src, dst, i, k):
         send(src, dst, rz_s.at[i, k], rz_r.at[i, k], to_z[1 - 2 * i])
 
+    def z_final(src, dst, c, i, k):
+        send(src, dst, rz_s.at[i, k], rf_r.at[i], to_z_core(1 - 2 * i, c))
+
     def rs_z_far(b):
         got(ry.at[3, 0:3, b], ry_r.at[3 + b])
         red[b, z2] = add(dkv[b, z2, y], ry[3, y1, b], ry[3, y3, b], ry[3, y2, b]).astype(BF)
@@ -304,29 +310,33 @@
     def rs_z_near():
         for i, z, c in ((2, z1, 0), (1, z3, 1)):
             y_sum(i)
-            z_send(red.at[:, z, 1 - c], rz.at[c, 1], c, 2)
+            z_final(red.at[:, z, 1 - c], rzf.at[c, core], 1 - c, c, 2)
 
     def rs_z_last(b):
         for c, z in enumerate((z1, z3)):
             got(rz.at[c, 0, b], rz_r.at[c, b])
             red[b, z, c] = add(red[b, z, c], rz[c, 0, b]).astype(BF)
-            z_send(red.at[b, z, c], rz.at[c, 2, b], c, 3 + b)
+            z_final(red.at[b, z, c], rzf.at[c, core, b], c, c, 3 + b)
+
+    def rs_pair():
+        y_sum(0)
+        send(red.at[:, zh, other], own.at[core], fin_s, fin_r, sib, False)
+        own[core] = red[:, zh, core]
 
     def rs_end():
-        for c in range(2):
-            got(rz.at[c, 1], rz_r.at[c, 2])
+        got(own.at[other], fin_r)
+        for i in range(2):
+            got(rzf.at[i], rf_r.at[i])
+        for h in range(2):
+            part = add(own[h], rzf[0, h], rzf[1, h])
             for b in range(2):
-                got(rz.at[c, 2, b], rz_r.at[c, 3 + b])
-        fin[0] = add(red[:, zh, 0], rz[0, 2], rz[1, 1])
-        fin[1] = add(red[:, zh, 1], rz[0, 1], rz[1, 2])
-        for t, out in enumerate((dk_out, dv_out)):
-            for b in range(2):
-                send(fin.at[other, b, t], out.at[:, block_cols(core, b)], fin_s, fin_r.at[t], sib, False)
-                keep(fin.at[core, b, t], out.at[:, block_cols(core, b)])
+                cols = slice(h * HALF + b * 128, h * HALF + b * 128 + 128)
+                fin[0, :, cols] = part[b, 0]
+                fin[1, :, cols] = part[b, 1]
+        keep(fin.at[0], dk_out)
+        keep(fin.at[1], dv_out)
 
     def rs_got():
-        for t, out in enumerate((dk_out, dv_out)):
-            got(out.at[:, theirs], fin_r.at[t])
         got(dq_out.at[:, theirs], dq_r)
 
     def w_start(b):
@@ -398,7 +408,7 @@
     rs_z_far(1)
     w_to_near()
     rs_z_near()
-    y_sum(0)
+    rs_pair()
     rs_z_last(0)
     rs_z_last(1)
     w_back()
@@ -411,7 +421,7 @@
     sent(kv.at[:, 0, 0:3], agz_s)
     sent(kv.at[:, 0:3], agy_s)
     sent(dkv.at[:, 0:3], ry_s)
-    sent(fin.at[0], fin_s)
+    sent(own.at[0], fin_s)
     sent(dqs.at[:, 0], dq_s)
     sent(w_a.at[0:15], a_s)
     sent(w_b.at[0:15], b_s)
@@ -468,9 +478,11 @@
             vm((2, 512, 128), BF),
             vm((2, 4, 4, 2, 2, LAT, 128), BF),
             vm((4, 4, 2, 2, 2, LAT, 128), BF),
-            vm((2, 3, 2, 2, LAT, 128), BF),
+            vm((2, 1, 2, 2, LAT, 128), BF),
+            vm((2, 2, 2, 2, LAT, 128), BF),
+            vm((2, 2, 2, LAT, 128), BF),
             vm((2, 4, 2, 2, LAT, 128), BF),
-            vm((2, 2, 2, LAT, 128), F32),
+            vm((2, LAT, D), F32),
             vm((2, 2, 128, 128), F32),
             vm((16, 16, D), BF),
             vm((16, 16, D), BF),
@@ -480,8 +492,8 @@
             vm((16, 16, D), BF),
             dma((11,)), dma((3,)), dma((3,)),
             dma, dma((10,)), dma, dma((5,)),
-            dma, dma((5,)), dma((2, 5)), dma((2, 5)),
-            dma, dma((2,)), dma, dma,
+            dma, dma((5,)), dma((2, 5)), dma((2, 2)), dma((2,)),
+            dma, dma, dma, dma,
             dma, dma, dma, dma, dma, dma, dma, dma, dma, dma,
         ],
         compiler_params=pltpu.CompilerParams(

time: 61.7 us -> 61.5 us (level)
  no operation moved by 1% of the time
where the time goes in v5:
time: 61.5 us; the launch traced here: 61.3 us
  Pallas kernels  60.7 us (99%)
  between operations  0.64 us (1%)
    pallas_call x1, Pallas kernels, shards(): pl.pallas_call(kernel, out_shape=[jax.ShapeDtypeStruct(i, F32) for i in s...  58.5 us
    pallas_call x1, Pallas kernels, shards(): pl.pallas_call(finish, out_shape=[jax.ShapeDtypeStruct(i, F32) for i in s...  2.13 us

profile of v5, /device:TPU:1, one launch (start us, length us, event | category | flops | bytes accessed | tf_op | source)
XLA Modules:
  0.0 61.3 jit_solution(17589479905320826905)
XLA Ops:
  0.6 58.5 %attend_back.1 = (f32[128,512]{1,0:T(8,128)}, f32[32,512]{1,0:T(8,128)}, f32[32,512]{1,0:T(8,128)}, bf16[2,16,16,512]{3,2,1,0:T(8,128)(2,1)}) custom-call(bf16[128,512]{1,0:T(8,128)(2,1)} %bitcast.10, bf16[32,512]{1,0:T(8,128)(2,1)} %bitcast.11, bf16[32,512]{1,0:T(8,128)(2,1)} %bitcast.12, bf16[512,512]{1,0:T(8,128)(2,1)} %w_hbm.1, f32[128,512]{1,0:T(8,128)} %bitcast.9), custom_call_target="tpu_custom_call" | custom-call | tf_op jit(solution)/shard_map/attend_back/pallas_call | solution.py:458
  59.2 2.1 %finish.1 = (f32[128,512]{1,0:T(8,128)}, f32[32,512]{1,0:T(8,128)}, f32[32,512]{1,0:T(8,128)}, f32[512,512]{1,0:T(8,128)}) custom-call(f32[128,512]{1,0:T(8,128)} %get-tuple-element.12.dq, f32[32,512]{1,0:T(8,128)} %get-tuple-element.13.dk, f32[32,512]{1,0:T(8,128)} %get-tuple-element.14.dv, bf16[512,512]{1,0:T(8,128)(2,1)} %bitcast.8), custom_call_target="tpu_custom_call" | custom-call | tf_op jit(solution)/shard_map/finish/pallas_call | solution.py:504

commit v6 on v5

--- a/solution.py
+++ b/solution.py
@@ -384,7 +384,6 @@
     def back(i):
         for b in range(2):
             backward(i, b, deltas[b])
-        rs_y(i)
 
     for i in range(3):
         got(kv.at[:, order[i], 0:3], agy_r.at[i])
@@ -403,15 +402,17 @@
         back(i)
     query_part(0)
     query_part(1)
+    for i in (2, 1, 0):
+        rs_y(i)
     w_to_line()
     rs_z_far(0)
     rs_z_far(1)
     w_to_near()
     rs_z_near()
-    rs_pair()
     rs_z_last(0)
     rs_z_last(1)
     w_back()
+    rs_pair()
     w_pair()
     rs_end()
     rs_got()

time: 61.5 us -> 62.5 us (1.016)
  Pallas kernels: 60.7 us -> 61.7 us
    pallas_call x1, Pallas kernels: 58.5 us -> 59.5 us  [shards(): pl.pallas_call(kernel, out_shape=[jax.ShapeDtypeStruct(i, F32) for i in s...]
where the time goes in v6:
time: 62.5 us; the launch traced here: 62.3 us
  Pallas kernels  61.7 us (99%)
  between operations  0.64 us (1%)
    pallas_call x1, Pallas kernels, shards(): pl.pallas_call(kernel, out_shape=[jax.ShapeDtypeStruct(i, F32) for i in s...  59.5 us
    pallas_call x1, Pallas kernels, shards(): pl.pallas_call(finish, out_shape=[jax.ShapeDtypeStruct(i, F32) for i in s...  2.13 us

profile of v6, /device:TPU:1, one launch (start us, length us, event | category | flops | bytes accessed | tf_op | source)
XLA Modules:
  0.0 62.3 jit_solution(15157692084924646322)
XLA Ops:
  0.6 59.5 %attend_back.1 = (f32[128,512]{1,0:T(8,128)}, f32[32,512]{1,0:T(8,128)}, f32[32,512]{1,0:T(8,128)}, bf16[2,16,16,512]{3,2,1,0:T(8,128)(2,1)}) custom-call(bf16[128,512]{1,0:T(8,128)(2,1)} %bitcast.10, bf16[32,512]{1,0:T(8,128)(2,1)} %bitcast.11, bf16[32,512]{1,0:T(8,128)(2,1)} %bitcast.12, bf16[512,512]{1,0:T(8,128)(2,1)} %w_hbm.1, f32[128,512]{1,0:T(8,128)} %bitcast.9), custom_call_target="tpu_custom_call" | custom-call | tf_op jit(solution)/shard_map/attend_back/pallas_call | solution.py:459
  60.2 2.1 %finish.1 = (f32[128,512]{1,0:T(8,128)}, f32[32,512]{1,0:T(8,128)}, f32[32,512]{1,0:T(8,128)}, f32[512,512]{1,0:T(8,128)}) custom-call(f32[128,512]{1,0:T(8,128)} %get-tuple-element.12.dq, f32[32,512]{1,0:T(8,128)} %get-tuple-element.13.dk, f32[32,512]{1,0:T(8,128)} %get-tuple-element.14.dv, bf16[512,512]{1,0:T(8,128)(2,1)} %bitcast.8), custom_call_target="tpu_custom_call" | custom-call | tf_op jit(solution)/shard_map/finish/pallas_call | solution.py:505

commit v7 on v5

--- a/solution.py
+++ b/solution.py
@@ -232,23 +232,40 @@
         ap[b, i, 0:64, :] = a[0:64, 0:256]
         ap[b, i, 64:128, :] = a[64:128, 256:512]
 
+    def joined(b, blocks):
+        top = tops[blocks[0]][b]
+        for i in blocks[1:]:
+            top = jnp.maximum(top, tops[i][b])
+        f = [jnp.exp2((tops[i][b] - top) * (SCALE * LOG2E)) for i in blocks]
+        total = f[0] * totals[blocks[0]][b]
+        for i, g in zip(blocks[1:], f[1:]):
+            total = total + g * totals[i][b]
+        return top, f, total
+
+    def weigh(b, blocks, f, h):
+        a = None
+        for i, g in zip(blocks, f):
+            part = ap[b, i, h * 64 : h * 64 + 64, :] * g[:, h * 256 : h * 256 + 256]
+            a = part if a is None else a + part
+        return a
+
+    def early(b):
+        top, f, total = joined(b, (0, 1, 2))
+        for h in range(2):
+            ap[b, 0, h * 64 : h * 64 + 64, :] = weigh(b, (0, 1, 2), f, h)
+        tops[0][b], totals[0][b] = top, total
+        for i in range(3):
+            gains[i][b] = f[i]
+
     def combine(b):
-        top = tops[0][b]
-        for i in range(1, 4):
-            top = jnp.maximum(top, tops[i][b])
-        f = [jnp.exp2((tops[i][b] - top) * (SCALE * LOG2E)) for i in range(4)]
-        total = f[0] * totals[0][b]
-        for i in range(1, 4):
-            total = total + f[i] * totals[i][b]
+        _, f, total = joined(b, (0, 3))
         inv = 1.0 / total
-        for i in range(4):
-            gains[i][b] = f[i] * inv
+        f = [g * inv for g in f]
+        for i in range(3):
+            gains[i][b] = gains[i][b] * f[0]
+        gains[3][b] = f[1]
         for h in range(2):
-            a = None
-            for i in range(4):
-                part = ap[b, i, h * 64 : h * 64 + 64, :] * gains[i][b][:, h * 256 : h * 256 + 256]
-                a = part if a is None else a + part
-            at[b * 128 + h * 64 : b * 128 + h * 64 + 64, :] = a.astype(BF)
+            at[b * 128 + h * 64 : b * 128 + h * 64 + 64, :] = weigh(b, (0, 3), f, h).astype(BF)
 
     def delta_of(b):
         cols = slice(b * 128, b * 128 + 128)
@@ -390,6 +407,8 @@
         got(kv.at[:, order[i], 0:3], agy_r.at[i])
         score(i, 0)
         score(i, 1)
+    early(0)
+    early(1)
     for b in range(2):
         got(kv.at[b, z2, 0:3], agy_r.at[3 + b])
         score(3, b)
@@ -408,10 +427,10 @@
     rs_z_far(1)
     w_to_near()
     rs_z_near()
-    rs_pair()
     rs_z_last(0)
     rs_z_last(1)
     w_back()
+    rs_pair()
     w_pair()
     rs_end()
     rs_got()

time: 61.5 us -> 62.4 us (1.015)
  Pallas kernels: 60.7 us -> 61.6 us
    pallas_call x1, Pallas kernels: 58.5 us -> 59.5 us  [shards(): pl.pallas_call(kernel, out_shape=[jax.ShapeDtypeStruct(i, F32) for i in s...]
where the time goes in v7:
time: 62.4 us; the launch traced here: 62.2 us
  Pallas kernels  61.6 us (99%)
  between operations  0.64 us (1%)
    pallas_call x1, Pallas kernels, shards(): pl.pallas_call(kernel, out_shape=[jax.ShapeDtypeStruct(i, F32) for i in s...  59.5 us
    pallas_call x1, Pallas kernels, shards(): pl.pallas_call(finish, out_shape=[jax.ShapeDtypeStruct(i, F32) for i in s...  2.13 us

profile of v7, /device:TPU:1, one launch (start us, length us, event | category | flops | bytes accessed | tf_op | source)
XLA Modules:
  0.0 62.2 jit_solution(6714969126816822394)
XLA Ops:
  0.6 59.5 %attend_back.1 = (f32[128,512]{1,0:T(8,128)}, f32[32,512]{1,0:T(8,128)}, f32[32,512]{1,0:T(8,128)}, bf16[2,16,16,512]{3,2,1,0:T(8,128)(2,1)}) custom-call(bf16[128,512]{1,0:T(8,128)(2,1)} %bitcast.10, bf16[32,512]{1,0:T(8,128)(2,1)} %bitcast.11, bf16[32,512]{1,0:T(8,128)(2,1)} %bitcast.12, bf16[512,512]{1,0:T(8,128)(2,1)} %w_hbm.1, f32[128,512]{1,0:T(8,128)} %bitcast.9), custom_call_target="tpu_custom_call" | custom-call | tf_op jit(solution)/shard_map/attend_back/pallas_call | solution.py:477
  60.1 2.1 %finish.1 = (f32[128,512]{1,0:T(8,128)}, f32[32,512]{1,0:T(8,128)}, f32[32,512]{1,0:T(8,128)}, f32[512,512]{1,0:T(8,128)}) custom-call(f32[128,512]{1,0:T(8,128)} %get-tuple-element.12.dq, f32[32,512]{1,0:T(8,128)} %get-tuple-element.13.dk, f32[32,512]{1,0:T(8,128)} %get-tuple-element.14.dv, bf16[512,512]{1,0:T(8,128)(2,1)} %bitcast.8), custom_call_target="tpu_custom_call" | custom-call | tf_op jit(solution)/shard_map/finish/pallas_call | solution.py:523

commit v8 on v5

--- a/solution.py
+++ b/solution.py
@@ -412,25 +412,26 @@
     rs_z_last(0)
     rs_z_last(1)
     w_back()
-    w_pair()
-    rs_end()
-    rs_got()
-    got(dw_out.at[other], e_r)
-
     sent(sub(zh, y, other), sib_s.at[0])
     sent(kv.at[:, 0, 0:3], agz_s)
     sent(kv.at[:, 0:3], agy_s)
     sent(dkv.at[:, 0:3], ry_s)
-    sent(own.at[0], fin_s)
     sent(dqs.at[:, 0], dq_s)
     sent(w_a.at[0:15], a_s)
     sent(w_b.at[0:15], b_s)
     sent(w_c.at[0:3], c_s)
+    rs_got()
+    w_pair()
+    last = sends.pop()
+    rs_end()
+    for c in sends:
+        c.wait_send()
+    sent(own.at[0], fin_s)
     sent(w_d.at[0:15], d_s)
+    got(dw_out.at[other], e_r)
+    last.wait_send()
     for c in kept:
         c.wait()
-    for c in sends:
-        c.wait_send()
 
 
 def finish(dq, dk, dv, dw, dq_out, dk_out, dv_out, dw_out, vq, vk, vv, half, full, sem):

time: 61.5 us -> 61.4 us (level)
  no operation moved by 1% of the time
where the time goes in v8:
time: 61.4 us; the launch traced here: 61.3 us
  Pallas kernels  60.6 us (99%)
  between operations  0.64 us (1%)
    pallas_call x1, Pallas kernels, shards(): pl.pallas_call(kernel, out_shape=[jax.ShapeDtypeStruct(i, F32) for i in s...  58.5 us
    pallas_call x1, Pallas kernels, shards(): pl.pallas_call(finish, out_shape=[jax.ShapeDtypeStruct(i, F32) for i in s...  2.13 us

profile of v8, /device:TPU:1, one launch (start us, length us, event | category | flops | bytes accessed | tf_op | source)
XLA Modules:
  0.0 61.3 jit_solution(10455723627613935733)
XLA Ops:
  0.6 58.5 %attend_back.1 = (f32[128,512]{1,0:T(8,128)}, f32[32,512]{1,0:T(8,128)}, f32[32,512]{1,0:T(8,128)}, bf16[2,16,16,512]{3,2,1,0:T(8,128)(2,1)}) custom-call(bf16[128,512]{1,0:T(8,128)(2,1)} %bitcast.10, bf16[32,512]{1,0:T(8,128)(2,1)} %bitcast.11, bf16[32,512]{1,0:T(8,128)(2,1)} %bitcast.12, bf16[512,512]{1,0:T(8,128)(2,1)} %w_hbm.1, f32[128,512]{1,0:T(8,128)} %bitcast.9), custom_call_target="tpu_custom_call" | custom-call | tf_op jit(solution)/shard_map/attend_back/pallas_call | solution.py:459
  59.1 2.1 %finish.1 = (f32[128,512]{1,0:T(8,128)}, f32[32,512]{1,0:T(8,128)}, f32[32,512]{1,0:T(8,128)}, f32[512,512]{1,0:T(8,128)}) custom-call(f32[128,512]{1,0:T(8,128)} %get-tuple-element.12.dq, f32[32,512]{1,0:T(8,128)} %get-tuple-element.13.dk, f32[32,512]{1,0:T(8,128)} %get-tuple-element.14.dv, bf16[512,512]{1,0:T(8,128)(2,1)} %bitcast.8), custom_call_target="tpu_custom_call" | custom-call | tf_op jit(solution)/shard_map/finish/pallas_call | solution.py:505
